TPU v7x, 128 devices: a whole 4x4x4 slice. The times are simulated.
128 devices in a mesh: gx: 4 (over x), gy: 4 (over y), gz: 8 (over z, core).
Axes of the slice: x: 4, y: 4, z: 4, core: 2. Of those that a mesh axis runs over, the one named last changes fastest.
Arguments:
- coarse_velocity: float32 [3, 64, 64, 1024], P(None, 'gx', 'gy', 'gz'), may hold values from -6 to 6
- coarse_viscosity: float32 [64, 64, 1024], P('gx', 'gy', 'gz'), may hold values from 0.1 to 3
- coarse_rhs: float32 [3, 64, 64, 1024], P(None, 'gx', 'gy', 'gz'), may hold values from -6 to 6
- fine_velocity: float32 [128, 4, 3, 32768], P(('gx', 'gy', 'gz')), may hold values from -6 to 6
- fine_rhs: float32 [128, 4, 3, 32768], P(('gx', 'gy', 'gz')), may hold values from -6 to 6
- fine_viscosity: float32 [128, 4, 32768], P(('gx', 'gy', 'gz')), may hold values from 0.1 to 3
- refined: int32 [128, 2], P(('gx', 'gy', 'gz')), may hold values from 0 to 7, as said below
- owner: int32 [128, 2], P(('gx', 'gy', 'gz')), may hold values from 0 to 127, as said below
Outputs:
- fine_out: float32 [128, 4, 3, 32768], P(('gx', 'gy', 'gz'))
- coarse_synced: float32 [3, 64, 64, 1024], P(None, 'gx', 'gy', 'gz')
- coarse_residual: float32 [3, 64, 64, 1024], P(None, 'gx', 'gy', 'gz')
Inputs may be any that keep to these rules, and one draw needn't show every extreme that they name: `refined`: each row holds 2 different positions. Row h names 2 different owners of home h's patches, all with the same indices along gy and gz as home h. Among the homes that share their indices along gy and gz, one owner is named in every row, so that all of its 4 slots hold patches.
All inputs are finite; a program needn't handle non-finite values.
Results may differ from a plain program's by a relative error of at most 0.00002.
Values sent between devices are 32-bit elements; how exact they have to be, the bound alone decides.
A program may use at most 192 MiB of HBM per device.

v0:
```python
import jax
import jax.numpy as jnp
import numpy as np
from jax import lax
from jax.sharding import PartitionSpec as P

PE = 32
SWEEPS = 2


reaction = 1.0


def with_halo(cells, sides, width):
    for axis, dim in sides:
        count = lax.axis_size(axis)
        ends = count - 1
        head = lax.slice_in_dim(cells, 0, width, axis=dim)
        tail = lax.slice_in_dim(cells, cells.shape[dim] - width, cells.shape[dim], axis=dim)
        cells = jnp.concatenate(
            [
                lax.ppermute(tail, axis, [(i, (i + 1) % count) for i in range(ends)]),
                cells,
                lax.ppermute(head, axis, [((i + 1) % count, i) for i in range(ends)]),
            ],
            axis=dim,
        )
    return cells


def patch_tables(patch_edge):
    cell_count = patch_edge * patch_edge * patch_edge
    numbers = np.arange(cell_count)
    position = (
        numbers // (patch_edge * patch_edge),
        numbers // patch_edge % patch_edge,
        numbers % patch_edge,
    )
    offsets = []
    inside = np.zeros((6, cell_count))
    for axis_number in range(3):
        stride = [patch_edge * patch_edge, patch_edge, 1][axis_number]
        for facing in range(2):
            direction = 2 * axis_number + facing
            offsets.append(stride if facing == 1 else -stride)
            at_border = position[axis_number] == (patch_edge - 1 if facing == 1 else 0)
            inside[direction] = np.where(at_border, 0.0, 1.0)
    colour = (position[0] + position[1] + position[2]) % 2 == 0
    return (offsets, inside, colour)


def rim_offsets(coarse_edge, stride_first, stride_second):
    offsets = []
    for axis_number in range(3):
        others = [index_value for index_value in range(3) if index_value != axis_number]
        for facing in range(2):
            layer_at = -1 if facing == 0 else coarse_edge
            for first_cell in range(coarse_edge):
                for second_cell in range(coarse_edge):
                    location = [0, 0, 0]
                    location[axis_number] = layer_at
                    location[others[0]] = first_cell
                    location[others[1]] = second_cell
                    offsets.append(
                        location[0] * stride_first + location[1] * stride_second + location[2]
                    )
    return np.array(offsets)


def cell_offsets(coarse_edge, stride_first, stride_second):
    offsets = []
    for first_cell in range(coarse_edge):
        for second_cell in range(coarse_edge):
            for third_cell in range(coarse_edge):
                offsets.append(first_cell * stride_first + second_cell * stride_second + third_cell)
    return np.array(offsets)


def shifted(values, offset):
    if offset > 0:
        filler = jnp.zeros(values.shape[:-1] + (offset,), values.dtype)
        return jnp.concatenate([values[..., offset:], filler], axis=-1)
    filler = jnp.zeros(values.shape[:-1] + (-offset,), values.dtype)
    return jnp.concatenate([filler, values[..., :offset]], axis=-1)


def neighbours(loaded, weights, offsets, state):
    total = loaded
    for direction in range(6):
        total = total + weights[direction][:, None, :] * shifted(state, offsets[direction])
    return total


def ghost_field(face, axis_number, facing):
    upsampled = jnp.repeat(jnp.repeat(face, 2, axis=1), 2, axis=2)
    upsampled = jnp.moveaxis(upsampled, 3, 1)
    widened = jnp.expand_dims(upsampled, 2 + axis_number)
    padding = [(0, 0), (0, 0), (0, 0), (0, 0), (0, 0)]
    padding[2 + axis_number] = (0, PE - 1) if facing == 0 else (PE - 1, 0)
    return jnp.pad(widened, padding).reshape(face.shape[0], 4, -1)


def smooth_patches(rim_values, velocity, forcing, viscosity):
    offsets, inside, colour = patch_tables(PE)
    slot_count = velocity.shape[0]
    coarse_edge = PE // 2
    faces = rim_values.reshape(slot_count, 6, coarse_edge, coarse_edge, 4)
    diagonal = jnp.full(viscosity.shape, reaction, jnp.float32)
    loaded = forcing
    weights = []
    for direction in range(6):
        ghost = ghost_field(faces[:, direction], direction // 2, direction % 2)
        interior = jnp.asarray(inside[direction], jnp.float32)
        face_weight = 0.5 * (
            viscosity + interior * shifted(viscosity, offsets[direction]) + ghost[:, 3]
        )
        diagonal = diagonal + face_weight
        loaded = loaded + face_weight[:, None, :] * ghost[:, :3]
        weights.append(face_weight * interior)
    red_cells = jnp.asarray(colour)
    state = velocity
    for sweep_number in range(SWEEPS):
        for parity in (red_cells, jnp.logical_not(red_cells)):
            update = neighbours(loaded, weights, offsets, state) / diagonal[:, None, :]
            state = jnp.where(parity, update, state)
    residual = neighbours(loaded, weights, offsets, state) - diagonal[:, None, :] * state
    joined = jnp.concatenate([residual, state], axis=1)
    blocks = joined.reshape(slot_count, 6, coarse_edge, 2, coarse_edge, 2, coarse_edge, 2)
    averaged = 0.125 * jnp.sum(blocks, axis=(3, 5, 7))
    return (state, averaged.reshape(slot_count, -1))


def coarse_residual(padded_velocity, padded_viscosity, rhs_values):
    middle = (slice(1, -1), slice(1, -1), slice(1, -1))
    centre_velocity = padded_velocity[(slice(None),) + middle]
    centre_viscosity = padded_viscosity[middle]
    applied = reaction * centre_velocity
    for axis_number in range(3):
        for step_size in (2, 0):
            window = list(middle)
            window[axis_number] = slice(step_size, step_size + centre_viscosity.shape[axis_number])
            window = tuple(window)
            face_weight = 0.5 * (centre_viscosity + padded_viscosity[window])
            applied = applied + 0.25 * face_weight * (
                centre_velocity - padded_velocity[(slice(None),) + window]
            )
    return rhs_values - applied


def shards(
    coarse_velocity,
    coarse_viscosity,
    coarse_rhs,
    fine_velocity,
    fine_rhs,
    fine_viscosity,
    refined,
    owner,
):
    coarse_edge = PE // 2
    size_first, size_second, size_third = coarse_viscosity.shape
    stacked = jnp.concatenate([coarse_velocity, coarse_viscosity[None]], axis=0)
    padded = with_halo(stacked, (("gx", 1), ("gy", 2), ("gz", 3)), 1)
    second_plane = size_second + 2
    third_plane = size_third + 2
    second_count = size_second // coarse_edge
    third_count = size_third // coarse_edge
    position = refined[0]
    owned_by = owner[0]
    patch_count = position.shape[0]
    first_anchor = position // (second_count * third_count) * coarse_edge
    second_anchor = position // third_count % second_count * coarse_edge
    third_anchor = position % third_count * coarse_edge
    base_index = (
        (first_anchor + 1) * (second_plane * third_plane)
        + (second_anchor + 1) * third_plane
        + third_anchor
        + 1
    )
    rim_table = jnp.asarray(
        rim_offsets(coarse_edge, second_plane * third_plane, third_plane), jnp.int32
    )
    rim_index = base_index[:, None] + rim_table[None, :]
    columns = padded.reshape(4, -1).T
    rim_values = columns[rim_index].reshape(patch_count, -1)
    patch_order = jnp.arange(patch_count, dtype=jnp.int32)
    earlier = (owned_by[None, :] == owned_by[:, None]) & (
        patch_order[None, :] < patch_order[:, None]
    )
    rank_in_row = jnp.sum(earlier.astype(jnp.int32), axis=1)
    owner_group = owned_by // (lax.axis_size("gy") * lax.axis_size("gz"))
    peer_count = lax.axis_size("gx")
    slot_count = fine_velocity.shape[1]
    capacity = slot_count // peer_count
    peer_order = jnp.arange(peer_count, dtype=jnp.int32)
    place_order = jnp.arange(capacity, dtype=jnp.int32)
    matches = (owner_group[None, None, :] == peer_order[:, None, None]) & (
        rank_in_row[None, None, :] == place_order[None, :, None]
    )
    present = jnp.any(matches, axis=2)
    source_patch = jnp.sum(matches.astype(jnp.int32) * patch_order[None, None, :], axis=2)
    outgoing = jnp.where(present[:, :, None], rim_values[source_patch], 0.0)
    arrived, arrived_flag = (
        lax.all_to_all(outgoing, "gx", split_axis=0, concat_axis=0, tiled=True),
        lax.all_to_all(present.astype(jnp.float32), "gx", split_axis=0, concat_axis=0, tiled=True),
    )
    smoothed, averaged = smooth_patches(
        arrived.reshape(slot_count, -1), fine_velocity[0], fine_rhs[0], fine_viscosity[0]
    )
    fine_out = smoothed * arrived_flag.reshape(slot_count)[:, None, None]
    returned = lax.all_to_all(
        averaged.reshape(peer_count, capacity, -1), "gx", split_axis=0, concat_axis=0, tiled=True
    )
    patch_average = returned[owner_group, rank_in_row]
    cell_base = (first_anchor * size_second + second_anchor) * size_third + third_anchor
    cell_table = jnp.asarray(
        cell_offsets(coarse_edge, size_second * size_third, size_third), jnp.int32
    )
    cell_index = (cell_base[:, None] + cell_table[None, :]).reshape(-1)
    split_average = patch_average.reshape(patch_count, 6, coarse_edge * coarse_edge * coarse_edge)
    mean_residual = jnp.moveaxis(split_average[:, :3], 1, 0).reshape(3, -1)
    mean_velocity = jnp.moveaxis(split_average[:, 3:], 1, 0).reshape(3, -1)
    synced = (
        coarse_velocity.reshape(3, -1)
        .at[:, cell_index]
        .set(mean_velocity)
        .reshape(coarse_velocity.shape)
    )
    padded_synced = with_halo(synced, (("gx", 1), ("gy", 2), ("gz", 3)), 1)
    residual = coarse_residual(padded_synced, padded[3], coarse_rhs)
    residual = (
        residual.reshape(3, -1).at[:, cell_index].set(mean_residual).reshape(coarse_rhs.shape)
    )
    return (fine_out[None], synced, residual)


def solution(mesh):
    return jax.shard_map(
        shards,
        mesh=mesh,
        in_specs=(
            P(None, "gx", "gy", "gz"),
            P("gx", "gy", "gz"),
            P(None, "gx", "gy", "gz"),
            P(("gx", "gy", "gz"), None, None, None),
            P(("gx", "gy", "gz"), None, None, None),
            P(("gx", "gy", "gz"), None, None),
            P(("gx", "gy", "gz"), None),
            P(("gx", "gy", "gz"), None),
        ),
        out_specs=(
            P(("gx", "gy", "gz"), None, None, None),
            P(None, "gx", "gy", "gz"),
            P(None, "gx", "gy", "gz"),
        ),
        check_vma=False,
    )
```

profile of v0, /device:TPU:1, one launch (start us, length us, event | category | flops | bytes accessed | tf_op | source)
XLA Modules:
  0.0 557.5 jit_solution(5650021186368625628)
XLA Ops:
  47.3 8.1 %pad_maximum_fusion = f32[4,18,18,128]{2,1,3,0:T(8,128)S(1)} fusion(f32[4,18,1,128]{2,1,3,0:T(8,128)} %copy.460, f32[4,18,16,128]{2,1,3,0:T(8,128)} %copy.459, f32[4,18,1,128]{2,1,3,0:T(8,128)} %copy.458), kind=kLoop, calls=%fused_computation.5 | loop fusion | flops 331776 | bytes 1327104 | tf_op jit(solution)/shard_map/concatenate | solution.py:20
  76.4 10.7 %copy.464 = f32[4,42120]{0,1:T(8,128)} copy(f32[4,42120]{1,0:T(4,128)S(1)} %reshape.582) | data formatting | bytes 1347840 | tf_op jit(solution)/shard_map/reshape | solution.py:184
  87.1 15.2 %gather_fusion = f32[3072,4]{1,0:T(8,128)S(1)} fusion(f32[42120,4]{1,0:T(8,128)} %bitcast.193, s32[3072]{0:T(1024)S(1)} %broadcast_clamp_fusion), kind=kCustom, calls=%fused_computation | custom fusion | bytes 110592 | tf_op jit(solution)/shard_map/gather | solution.py:185
  128.8 8.9 %pad.65.clone = f32[4,4,32,32,32]{4,3,2,1,0:T(8,128)} pad(f32[4,4,32,32,1]{4,3,2,1,0:T(8,128)} %copy.544, f32[]{:T(128)} %constant.100.clone.1), padding=0_0x0_0x0_0x0_0x31_0 | pad | bytes 2162692 | tf_op jit(solution)/shard_map/jit(_pad)/pad | solution.py:100
  137.7 6.2 %reshape.601 = f32[4,4,32768]{2,1,0:T(4,128)S(1)} reshape(f32[4,4,32,32,32]{4,3,2,1,0:T(8,128)} %pad.65.clone) | data formatting | bytes 4194304 | tf_op jit(solution)/shard_map/reshape | solution.py:100
  153.3 7.2 %reshape.586 = f32[4,4,32768]{2,1,0:T(4,128)} reshape(f32[4,4,32,32,32]{4,3,2,1,0:T(8,128)} %pad.60.clone) | data formatting | bytes 4194304 | tf_op jit(solution)/shard_map/reshape | solution.py:100
  171.4 7.3 %reshape.589 = f32[4,4,32768]{2,1,0:T(4,128)} reshape(f32[4,4,32,32,32]{4,3,2,1,0:T(8,128)} %pad.61.clone) | data formatting | bytes 4194304 | tf_op jit(solution)/shard_map/reshape | solution.py:100
  189.8 7.2 %reshape.592 = f32[4,4,32768]{2,1,0:T(4,128)} reshape(f32[4,4,32,32,32]{4,3,2,1,0:T(8,128)} %pad.62.clone) | data formatting | bytes 4194304 | tf_op jit(solution)/shard_map/reshape | solution.py:100
  208.8 8.1 %pad.64.clone = f32[4,4,32,32,32]{4,3,2,1,0:T(8,128)} pad(f32[4,4,32,32,1]{4,3,2,1,0:T(8,128)} %copy.543, f32[]{:T(128)} %constant.100.clone.1), padding=0_0x0_0x0_0x0_0x0_31 | pad | bytes 2162692 | tf_op jit(solution)/shard_map/jit(_pad)/pad | solution.py:100
  216.9 7.2 %reshape.598 = f32[4,4,32768]{2,1,0:T(4,128)} reshape(f32[4,4,32,32,32]{4,3,2,1,0:T(8,128)} %pad.64.clone) | data formatting | bytes 4194304 | tf_op jit(solution)/shard_map/reshape | solution.py:100
  232.5 7.5 %reshape.595 = f32[4,4,32768]{2,1,0:T(4,128)} reshape(f32[4,4,32,32,32]{4,3,2,1,0:T(8,128)} %pad.63.clone) | data formatting | bytes 4194304 | tf_op jit(solution)/shard_map/reshape | solution.py:100
  252.8 12.4 %divide_select_fusion.3 = (f32[4,3,32768]{2,1,0:T(4,128)S(1)}, f32[4,3,32768]{2,1,0:T(4,128)S(1)}) fusion(f32[4,3,32767]{2,1,0:T(4,128)S(1)} %copy-done.11, f32[4,3,32767]{2,1,0:T(4,128)S(1)} %copy-done.10, f32[4,3,32736]{2,1,0:T(4,128)S(1)} %copy-done.9, f32[4,3,32736]{2,1,0:T(4,128)S(1)} %copy-done.8, f32[4,3,31744]{2,1,0:T(4,128)} %get-tuple-element.82, ...), kind=kLoop, calls=%fused_computation.10 | loop fusion | flops 10223616 | bytes 31912864 | tf_op jit(solution)/shard_map/jit(_where)/select_n | solution.py:125
  287.6 6.5 %multiply_bitcast_fusion = (f32[1,4,3,32768]{3,2,1,0:T(4,128)}, f32[4,3,32768]{2,1,0:T(4,128)S(1)}) fusion(f32[4]{0:T(128)S(1)} %reduce.3, f32[4,3,32768]{2,1,0:T(4,128)S(1)} %divide_select_fusion.1, f32[4,32768]{1,0:T(4,128)S(1)} %get-tuple-element.92, f32[4,3,32767]{2,1,0:T(4,128)S(1)} %get-tuple-element.68, f32[4,32768]{1,0:T(4,128)S(1)} %get-tuple-element.47, ...), kind=kLoop, calls=%fused_computation.25 | loop fusion | flops 5898240 | bytes 19329968 | tf_op jit(solution)/shard_map/broadcast_in_dim | solution.py:234
  306.0 30.8 %copy.494 = f32[4,6,32768]{1,2,0:T(8,128)} copy(f32[4,6,32768]{2,1,0:T(8,128)} %pad_maximum_fusion.1) | data formatting | bytes 6291456 | tf_op jit(solution)/shard_map/concatenate | solution.py:127
  336.8 49.4 %reduce_sum.34 = f32[4,6,16,16,16]{1,4,3,2,0:T(8,128)} reduce(f32[4,6,16,2,16,2,16,2]{1,7,6,5,4,3,2,0:T(2,128)} %bitcast.49, f32[]{:T(128)} %constant.100.clone.1), dimensions={3,5,7}, to_apply=%region_3.4 | reduce | flops 688128 | bytes 3538948 | tf_op jit(solution)/shard_map/reduce_sum | solution.py:129
  386.2 10.6 %copy.495 = f32[4,6,16,16,16]{4,3,2,1,0:T(8,128)} copy(f32[4,6,16,16,16]{1,4,3,2,0:T(8,128)} %reduce_sum.34) | data formatting | bytes 786432 | tf_op jit(solution)/shard_map/reduce_sum | solution.py:129
  405.4 8.7 %copy.493 = f32[3,16,16,128]{0,3,2,1:T(8,128)} copy(f32[3,16,16,128]{3,2,1,0:T(8,128)S(1)} %copy-done.16) | data formatting | bytes 786432 | tf_op args[0]
  417.9 32.3 %scatter_fusion = f32[3,32768]{0,1:T(8,128)} fusion(f32[3,32768]{0,1:T(8,128)} %bitcast.185, s32[8192]{0:T(1024)S(1)} %bitcast.215, f32[8192,3]{1,0:T(8,128)} %copy.497), kind=kCustom, calls=%fused_computation.3 | custom fusion | bytes 327680 | tf_op jit(solution)/shard_map/scatter | solution.py:226
  450.2 10.0 %copy.528 = f32[3,16,16,128]{3,2,1,0:T(8,128)S(1)} copy(f32[3,16,16,128]{0,3,2,1:T(8,128)} %bitcast.186) | data formatting | bytes 786432
  465.5 10.0 %copy.503 = f32[3,16,16,128]{3,1,2,0:T(8,128)S(1)} copy(f32[3,16,16,128]{0,3,2,1:T(8,128)} %bitcast.187) | data formatting | bytes 786432 | tf_op jit(solution)/shard_map/reshape | solution.py:227
  489.5 6.4 %collective-permute-start.11 = (f32[3,18,18,1]{2,1,3,0:T(8,128)}, f32[3,18,18,1]{2,1,3,0:T(8,128)}, u32[]{:S(2)}, u32[]{:S(2)}) collective-permute-start(f32[3,18,18,1]{2,1,3,0:T(8,128)} %copy.521), channel_id=1, source_target_pairs={{0,1},{1,2},{2,3},{3,4},{4,5},{5,6},{6,7},{8,9},{9,10},{10,11},{11... | collective-permute-start | bytes 11672 | tf_op jit(solution)/shard_map/ppermute | solution.py:22
  505.6 8.6 %copy.525 = f32[3,16,16,128]{0,3,2,1:T(8,128)} copy(f32[3,16,16,128]{3,1,2,0:T(8,128)S(1)} %fusion.14) | data formatting | bytes 786432 | tf_op jit(solution)/shard_map/sub | solution.py:147
  514.3 32.3 %scatter_fusion.1 = f32[3,32768]{0,1:T(8,128)} fusion(f32[3,32768]{0,1:T(8,128)} %bitcast.191, s32[8192]{0:T(1024)S(1)} %bitcast.216, f32[8192,3]{1,0:T(8,128)} %copy.526), kind=kCustom, calls=%fused_computation.4 | custom fusion | bytes 327680 | tf_op jit(solution)/shard_map/scatter | solution.py:232
  546.6 10.6 %copy.529 = f32[3,16,16,128]{3,2,1,0:T(8,128)} copy(f32[3,16,16,128]{0,3,2,1:T(8,128)} %bitcast.192) | data formatting | bytes 786432
  (240 shorter events, 233.4 us)
Async XLA Ops:
  0.6 16.4 %copy-start = (f32[1,4,32768]{2,1,0:T(4,128)S(1)}, f32[1,4,32768]{2,1,0:T(4,128)}, u32[]{:S(2)}) copy-start(f32[1,4,32768]{2,1,0:T(4,128)} %param.22) | copy-start | bytes 1572868
  1.5 28.6 %collective-permute-start = (f32[4,1,16,128]{3,2,1,0:T(8,128)S(1)}, f32[4,1,16,128]{3,2,1,0:T(8,128)S(1)}, u32[]{:S(2)}, u32[]{:S(2)}) collective-permute-start(f32[4,1,16,128]{3,2,1,0:T(8,128)S(1)} %get-tuple-element.112), channel_id=1, source_target_pairs={{0,32},{32,64},{64,96},{1,33},{33,65},{65,97},{2,34},{34,66},{66,9... | collective-permute-start | bytes 98312 | tf_op jit(solution)/shard_map/ppermute | solution.py:22
  5.4 24.6 %collective-permute-start.1 = (f32[4,1,16,128]{3,2,1,0:T(8,128)S(1)}, f32[4,1,16,128]{3,2,1,0:T(8,128)S(1)}, u32[]{:S(2)}, u32[]{:S(2)}) collective-permute-start(f32[4,1,16,128]{3,2,1,0:T(8,128)S(1)} %get-tuple-element.113), channel_id=1, source_target_pairs={{32,0},{64,32},{96,64},{33,1},{65,33},{97,65},{34,2},{66,34},{98,6... | collective-permute-start | bytes 98312 | tf_op jit(solution)/shard_map/ppermute | solution.py:24
  9.7 95.2 %all-to-all-start.1 = ((f32[4,1,1]{2,1,0:T(1,128)}), f32[4,1,1]{2,1,0:T(1,128)S(1)}, u32[]{:S(2)}, u32[]{:S(2)}) async-start(f32[4,1,1]{2,1,0:T(1,128)} %copy.492), calls=%async_computation.1 | async-start | bytes 4096 | tf_op jit(solution)/shard_map/all_to_all | solution.py:205
  30.2 8.8 %collective-permute-start.2 = (f32[4,18,1,128]{3,1,2,0:T(8,128)S(1)}, f32[4,18,1,128]{3,1,2,0:T(8,128)S(1)}, u32[]{:S(2)}, u32[]{:S(2)}) collective-permute-start(f32[4,18,1,128]{3,1,2,0:T(8,128)S(1)} %copy.532), channel_id=1, source_target_pairs={{0,8},{8,16},{16,24},{1,9},{9,17},{17,25},{2,10},{10,18},{18,26},{... | collective-permute-start | bytes 110600 | tf_op jit(solution)/shard_map/ppermute | solution.py:22
  33.4 9.7 %collective-permute-start.3 = (f32[4,18,1,128]{3,1,2,0:T(8,128)S(1)}, f32[4,18,1,128]{3,1,2,0:T(8,128)S(1)}, u32[]{:S(2)}, u32[]{:S(2)}) collective-permute-start(f32[4,18,1,128]{3,1,2,0:T(8,128)S(1)} %copy.533), channel_id=1, source_target_pairs={{8,0},{16,8},{24,16},{9,1},{17,9},{25,17},{10,2},{18,10},{26,18},{... | collective-permute-start | bytes 110600 | tf_op jit(solution)/shard_map/ppermute | solution.py:24
  58.1 12.2 %collective-permute-start.4 = (f32[4,18,18,1]{2,1,3,0:T(8,128)S(1)}, f32[4,18,18,1]{2,1,3,0:T(8,128)S(1)}, u32[]{:S(2)}, u32[]{:S(2)}) collective-permute-start(f32[4,18,18,1]{2,1,3,0:T(8,128)S(1)} %get-tuple-element.49), channel_id=1, source_target_pairs={{0,1},{1,2},{2,3},{3,4},{4,5},{5,6},{6,7},{8,9},{9,10},{10,11},{11... | collective-permute-start | bytes 15560 | tf_op jit(solution)/shard_map/ppermute | solution.py:22
  63.3 8.5 %collective-permute-start.5 = (f32[4,18,18,1]{2,1,3,0:T(8,128)S(1)}, f32[4,18,18,1]{2,1,3,0:T(8,128)S(1)}, u32[]{:S(2)}, u32[]{:S(2)}) collective-permute-start(f32[4,18,18,1]{2,1,3,0:T(8,128)S(1)} %get-tuple-element.50), channel_id=1, source_target_pairs={{1,0},{2,1},{3,2},{4,3},{5,4},{6,5},{7,6},{9,8},{10,9},{11,10},{12... | collective-permute-start | bytes 15560 | tf_op jit(solution)/shard_map/ppermute | solution.py:24
  75.4 11.6 %copy-start.7 = (f32[4,18,18,130]{3,2,1,0:T(8,128)}, f32[4,18,18,130]{3,2,1,0:T(8,128)S(1)}, u32[]{:S(2)}) copy-start(f32[4,18,18,130]{3,2,1,0:T(8,128)S(1)} %pad_maximum_fusion.2) | copy-start | bytes 2021764
  104.9 9.2 %all-to-all-start = ((f32[4,1,6144]{2,1,0:T(1,128)}), f32[4,1,6144]{2,1,0:T(1,128)S(1)}, u32[]{:S(2)}, u32[]{:S(2)}) async-start(f32[4,1,6144]{2,1,0:T(1,128)} %copy.465), calls=%async_computation | async-start | bytes 196608 | tf_op jit(solution)/shard_map/all_to_all | solution.py:204
  232.5 9.7 %copy-start.21 = (f32[4,1,32768]{2,1,0:T(1,128)S(1)}, f32[4,1,32768]{2,1,0:T(1,128)}, u32[]{:S(2)}) copy-start(f32[4,1,32768]{2,1,0:T(1,128)} %slice.362) | copy-start | bytes 1572868
  232.5 12.5 %copy-start.28 = (f32[32768]{0:T(1024)S(1)}, f32[32768]{0:T(1024)}, u32[]{:S(2)}) copy-start(f32[32768]{0:T(1024)} %constant.121.clone) | copy-start | bytes 393220
  232.5 12.5 %copy-start.29 = (f32[32768]{0:T(1024)S(1)}, f32[32768]{0:T(1024)}, u32[]{:S(2)}) copy-start(f32[32768]{0:T(1024)} %constant.122.clone) | copy-start | bytes 393220
  232.5 12.5 %copy-start.30 = (f32[32768]{0:T(1024)S(1)}, f32[32768]{0:T(1024)}, u32[]{:S(2)}) copy-start(f32[32768]{0:T(1024)} %constant.123.clone) | copy-start | bytes 393220
  400.9 13.2 %all-to-all-start.2 = ((f32[4,1,24576]{2,1,0:T(1,128)}), f32[4,1,24576]{2,1,0:T(1,128)S(1)}, u32[]{:S(2)}, u32[]{:S(2)}) async-start(f32[4,1,24576]{2,1,0:T(1,128)} %mul.641), calls=%async_computation.2 | async-start | bytes 786432 | tf_op jit(solution)/shard_map/all_to_all | solution.py:211
  405.4 12.5 %copy-start.24 = (s32[8192,1]{0,1:T(1,128)}, s32[8192,1]{0,1:T(1,128)S(1)}, u32[]{:S(2)}) copy-start(s32[8192,1]{0,1:T(1,128)S(1)} %compare_select_fusion) | copy-start | bytes 98308
  460.2 15.3 %copy-start.23 = (f32[3,16,16,128]{3,2,1,0:T(8,128)}, f32[3,16,16,128]{3,2,1,0:T(8,128)S(1)}, u32[]{:S(2)}) copy-start(f32[3,16,16,128]{3,2,1,0:T(8,128)S(1)} %copy.528) | copy-start | bytes 1179652
  460.2 15.3 %collective-permute-start.6 = (f32[3,1,16,128]{3,2,1,0:T(8,128)S(1)}, f32[3,1,16,128]{3,2,1,0:T(8,128)S(1)}, u32[]{:S(2)}, u32[]{:S(2)}) collective-permute-start(f32[3,1,16,128]{3,2,1,0:T(8,128)S(1)} %get-tuple-element.123), channel_id=1, source_target_pairs={{32,0},{64,32},{96,64},{33,1},{65,33},{97,65},{34,2},{66,34},{98,6... | collective-permute-start | bytes 73736 | tf_op jit(solution)/shard_map/ppermute | solution.py:24
  461.5 14.0 %collective-permute-start.7 = (f32[3,1,16,128]{3,2,1,0:T(8,128)S(1)}, f32[3,1,16,128]{3,2,1,0:T(8,128)S(1)}, u32[]{:S(2)}, u32[]{:S(2)}) collective-permute-start(f32[3,1,16,128]{3,2,1,0:T(8,128)S(1)} %get-tuple-element.122), channel_id=1, source_target_pairs={{0,32},{32,64},{64,96},{1,33},{33,65},{65,97},{2,34},{34,66},{66,9... | collective-permute-start | bytes 73736 | tf_op jit(solution)/shard_map/ppermute | solution.py:22
  475.6 7.3 %collective-permute-start.8 = (f32[3,18,1,128]{3,1,2,0:T(8,128)S(1)}, f32[3,18,1,128]{3,1,2,0:T(8,128)S(1)}, u32[]{:S(2)}, u32[]{:S(2)}) collective-permute-start(f32[3,18,1,128]{3,1,2,0:T(8,128)S(1)} %get-tuple-element.121), channel_id=1, source_target_pairs={{8,0},{16,8},{24,16},{9,1},{17,9},{25,17},{10,2},{18,10},{26,18},{... | collective-permute-start | bytes 82952 | tf_op jit(solution)/shard_map/ppermute | solution.py:24
  476.9 6.0 %collective-permute-start.9 = (f32[3,18,1,128]{3,1,2,0:T(8,128)S(1)}, f32[3,18,1,128]{3,1,2,0:T(8,128)S(1)}, u32[]{:S(2)}, u32[]{:S(2)}) collective-permute-start(f32[3,18,1,128]{3,1,2,0:T(8,128)S(1)} %get-tuple-element.120), channel_id=1, source_target_pairs={{0,8},{8,16},{16,24},{1,9},{9,17},{17,25},{2,10},{10,18},{18,26},{... | collective-permute-start | bytes 82952 | tf_op jit(solution)/shard_map/ppermute | solution.py:22
  485.2 11.3 %copy-start.12 = (f32[1,4,3,32768]{3,2,1,0:T(4,128)S(1)}, f32[1,4,3,32768]{3,2,1,0:T(4,128)}, u32[]{:S(2)}) copy-start(f32[1,4,3,32768]{3,2,1,0:T(4,128)} %get-tuple-element.33) | copy-start | bytes 4718596
  485.2 16.1 %collective-permute-start.10 = (f32[3,18,18,1]{2,1,3,0:T(8,128)}, f32[3,18,18,1]{2,1,3,0:T(8,128)}, u32[]{:S(2)}, u32[]{:S(2)}) collective-permute-start(f32[3,18,18,1]{2,1,3,0:T(8,128)} %copy.517), channel_id=1, source_target_pairs={{1,0},{2,1},{3,2},{4,3},{5,4},{6,5},{7,6},{9,8},{10,9},{11,10},{12... | collective-permute-start | bytes 11672 | tf_op jit(solution)/shard_map/ppermute | solution.py:24
  489.5 13.2 %collective-permute-start.11 = (f32[3,18,18,1]{2,1,3,0:T(8,128)}, f32[3,18,18,1]{2,1,3,0:T(8,128)}, u32[]{:S(2)}, u32[]{:S(2)}) collective-permute-start(f32[3,18,18,1]{2,1,3,0:T(8,128)} %copy.521), channel_id=1, source_target_pairs={{0,1},{1,2},{2,3},{3,4},{4,5},{5,6},{6,7},{8,9},{9,10},{10,11},{11... | collective-permute-start | bytes 11672 | tf_op jit(solution)/shard_map/ppermute | solution.py:22
  (30 other events, 136.8 us)
where the time goes:
time: 568 us; the launch traced here: 557 us
  local copies, waits for them, and re-layouts  385 us (68%)
  other arithmetic  116 us (20%)
  starting transfers between devices  50.4 us (9%)
    unnamed x92, local copies, waits for them, and re-layouts  52.2 us
    reduce_sum x1, other arithmetic, smooth_patches(): averaged = 0.125 * jnp.sum(blocks, axis=(3, 5, 7))  49.4 us
    reshape x6, local copies, waits for them, and re-layouts, ghost_field(): return jnp.pad(widened, padding).reshape(face.shape[0], 4, -1)  42.4 us
    pad x6, local copies, waits for them, and re-layouts, ghost_field(): return jnp.pad(widened, padding).reshape(face.shape[0], 4, -1)  34.6 us
    scatter x1, local copies, waits for them, and re-layouts, shards(): synced = coarse_velocity.reshape(3, -1).at[:, cell_index].set(mean_veloci...  32.3 us
    scatter x1, local copies, waits for them, and re-layouts, shards(): residual.reshape(3, -1).at[:, cell_index].set(mean_residual)  32.3 us
    concatenate x1, local copies, waits for them, and re-layouts, smooth_patches(): joined = jnp.concatenate([residual, state], axis=1)  30.8 us
    ppermute x6, starting transfers between devices, with_halo(): lax.ppermute(tail, axis, [(i, (i + 1) % count) for i in range(ends)])  27.7 us
  transfers between devices with their start and end apart: 15, of which 1 were waited for; matrix products, arithmetic and copies ran while one was open for 19% of the time, Pallas kernels for 0%

commit v1 on v0

v1 whole, which is shorter than its diff:
```python
import functools

import jax
import jax.numpy as jnp
from jax import lax
from jax.experimental import pallas as pl
from jax.experimental.pallas import tpu as pltpu
from jax.sharding import PartitionSpec as P

SWEEPS = 2
EDGE = 16
SLOTS = 4
REACTION = 1.0
TILE = (8, 128)
SLAB = (16, 128)
MESH = pl.DeviceIdType.MESH
AXES = ("gx", "gy", "gz")


def lane_take(values, index):
    numbers = lax.GatherDimensionNumbers(
        offset_dims=(),
        collapsed_slice_dims=(1,),
        start_index_map=(1,),
        operand_batching_dims=(0,),
        start_indices_batching_dims=(0,),
    )
    return lax.gather(
        values,
        index[..., None],
        numbers,
        slice_sizes=(1, 1),
        mode=lax.GatherScatterMode.PROMISE_IN_BOUNDS,
    )


def push(source, target, sent, landed, device):
    return pltpu.make_async_remote_copy(
        src_ref=source,
        dst_ref=target,
        send_sem=sent,
        recv_sem=landed,
        device_id=device,
        device_id_type=MESH,
    )


def kernel(
    cv, cm, cr, fv, fr, fm, place, own,
    fo, so, ro,
    C, CR, FV, FR, FM, HX, HY, HZ, EF, ZF, MSG, RIM, PV, U, LD, W, GY, RB,
    MEAN, RET, SP, RM, HX2, HY2, HZ2, ZF2,
    lsem, asend, arecv, bsend, brecv, csend, crecv, dsend, drecv,
):
    at = [lax.axis_index(axis) for axis in AXES]
    size = [lax.axis_size(axis) for axis in AXES]
    me, peers = at[0], size[0]

    def beside(number, step):
        return {AXES[number]: lax.rem(at[number] + (step + size[number]), size[number])}

    loads = [
        pltpu.make_async_copy(cv, C.at[0:3, 1 : EDGE + 1], lsem.at[0]),
        pltpu.make_async_copy(cm, C.at[3, 1 : EDGE + 1], lsem.at[1]),
        pltpu.make_async_copy(fm, FM, lsem.at[2]),
        pltpu.make_async_copy(fr, FR, lsem.at[3]),
        pltpu.make_async_copy(fv, FV, lsem.at[4]),
        pltpu.make_async_copy(cr, CR, lsem.at[5]),
    ]
    for load in loads:
        load.start()

    barrier = pltpu.get_barrier_semaphore()
    for step in range(1, peers):
        pl.semaphore_signal(barrier, inc=1, device_id=beside(0, step), device_id_type=MESH)
    for number in (1, 2):
        for step in (1, -1):
            pl.semaphore_signal(
                barrier, inc=1, device_id=beside(number, step), device_id_type=MESH
            )
    pl.semaphore_wait(barrier, peers + 3)

    lane = lax.broadcasted_iota(jnp.int32, TILE, 1)
    row = lax.broadcasted_iota(jnp.int32, TILE, 0)
    third = lane & 31
    quarter = lane >> 5
    even = ((third + quarter) & 1) == 0
    z_first, z_last = third == 0, third == 31
    y_first = (row == 0) & (quarter == 0)
    y_last = (row == 7) & (quarter == 3)
    lane16 = lax.broadcasted_iota(jnp.int32, SLAB, 1)
    row16 = lax.broadcasted_iota(jnp.int32, SLAB, 0)
    group16 = lane16 >> 4
    inner16 = lane16 & 15
    positions = [place[0, 0], place[0, 1]]
    groups = [lax.div(own[0, i], size[1] * size[2]) for i in range(2)]

    def faces(block, planes, hx, hy, hz, packed, sent, landed):
        first, last = 1, EDGE
        return [
            push(block.at[:, last], hx.at[0], sent.at[0], landed.at[0], beside(0, 1)),
            push(block.at[:, first], hx.at[1], sent.at[1], landed.at[1], beside(0, -1)),
            push(block.at[:, planes, EDGE - 1], hy.at[0], sent.at[2], landed.at[2], beside(1, 1)),
            push(block.at[:, planes, 0], hy.at[1], sent.at[3], landed.at[3], beside(1, -1)),
            push(packed, hz.at[0], sent.at[4], landed.at[4], beside(2, 1)),
            push(packed, hz.at[1], sent.at[5], landed.at[5], beside(2, -1)),
        ]

    loads[0].wait()
    loads[1].wait()
    outward = faces(C, pl.ds(1, EDGE), HX, HY, HZ, ZF, asend, arecv)
    for copy in outward[:4]:
        copy.start()
    packed = jnp.zeros(SLAB, jnp.float32)
    for c in range(4):
        upper = jnp.zeros(SLAB, jnp.float32)
        lower = jnp.zeros(SLAB, jnp.float32)
        for x in range(EDGE):
            plane = C[c, x + 1]
            here = inner16 == x
            upper = jnp.where(here, pltpu.roll(plane, (x - 15) % 128, 1), upper)
            lower = jnp.where(here, pltpu.roll(plane, x, 1), lower)
        EF[0, c] = upper
        EF[1, c] = lower
        turn = (32 * c + 16) % 128
        packed = jnp.where(group16 == 2 * c, pltpu.roll(upper, turn, 1), packed)
        packed = jnp.where(group16 == 2 * c + 1, pltpu.roll(lower, turn, 1), packed)
    ZF[...] = packed
    for copy in outward[4:]:
        copy.start()

    loads[2].wait()
    loads[3].wait()
    loads[4].wait()

    def pack(j, carry):
        def pair(ref, start):
            low = ref[pl.ds(start + 64 * j, 8, stride=SLOTS), :]
            high = ref[pl.ds(start + 64 * j + 32, 8, stride=SLOTS), :]
            return jnp.where(even, low, high), jnp.where(even, high, low)

        for s in range(SLOTS):
            PV[s, 0, j + 1], PV[s, 1, j + 1] = pair(FM, s)
            for c in range(3):
                LD[s, 0, c, j], LD[s, 1, c, j] = pair(FR, c * 1024 + s)
                U[s, 0, c, j + 1], U[s, 1, c, j + 1] = pair(FV, c * 1024 + s)
        return carry

    lax.fori_loop(0, EDGE, pack, 0)

    for copy in outward:
        copy.wait_recv()
    for number, halo in ((0, HX), (1, HY)):
        for facing in range(2):
            outside = at[number] == (size[number] - 1 if facing else 0)
            halo[facing] = jnp.where(outside, 0.0, halo[facing])
    for facing in range(2):
        outside = at[2] == (size[2] - 1 if facing else 0)
        HZ[facing] = jnp.where(outside, 0.0, HZ[facing])

    odd_group = (group16 & 1) == 1
    across = jnp.where(odd_group, HZ[1], HZ[0])
    rims = []
    for i in range(2):
        p = positions[i]
        parts = [jnp.zeros(SLAB, jnp.float32)] * 3
        for c in range(4):
            for facing in range(2):
                g = 2 * c + facing
                here = group16 == g
                turn = (16 * g - 16 * p) & 127
                turn_z = (16 * g - 16 * p + (-16 if facing else 16)) & 127
                parts = [
                    jnp.where(here, pltpu.roll(HX[facing, c], turn, 1), parts[0]),
                    jnp.where(here, pltpu.roll(HY[facing, c], turn, 1), parts[1]),
                    jnp.where(here, pltpu.roll(EF[facing, c], turn_z, 1), parts[2]),
                ]
        parts[2] = jnp.where(jnp.where(odd_group, p - 7, p) == 0, across, parts[2])
        rims.append(parts)
    for peer in range(peers):
        is_first = jnp.full(SLAB, groups[0], jnp.int32) == peer
        for k in range(3):
            MSG[peer, 16 * k : 16 * k + 16] = jnp.where(is_first, rims[0][k], rims[1][k])
        first = jnp.full(TILE, groups[0], jnp.int32) == peer
        second = jnp.full(TILE, groups[1], jnp.int32) == peer
        MSG[peer, 48:56] = jnp.where(first | second, 1.0, 0.0)
    out_rims = []
    for step in range(1, peers):
        peer = lax.rem(me + step, peers)
        out_rims.append(
            push(
                MSG.at[peer], RIM.at[me], bsend.at[step - 1], brecv.at[step - 1], beside(0, step)
            )
        )
        out_rims[-1].start()
    RIM[me] = MSG[me]

    def y_up(tile):
        turned = pltpu.roll(tile, 96, 1)
        return jnp.where(quarter == 3, pltpu.roll(turned, 7, 0), turned)

    def y_down(tile):
        turned = pltpu.roll(tile, 32, 1)
        return jnp.where(quarter == 0, pltpu.roll(turned, 1, 0), turned)

    def far(colour, before, after):
        if colour == 0:
            return jnp.where(even, before, after)
        return jnp.where(even, after, before)

    def total(s, colour, c, j, weights):
        other = U.at[s, 1 - colour, c]
        tile = other[j + 1]
        return (
            LD[s, colour, c, j]
            + weights[0] * tile
            + weights[1] * far(colour, other[j], other[j + 2])
            + weights[2] * y_down(tile)
            + weights[3] * y_up(tile)
            + weights[4] * pltpu.roll(tile, 1, 1)
            + weights[5] * pltpu.roll(tile, 127, 1)
        )

    def one_slot(turn, carry):
        s = lax.rem(me + (2 * peers - turn), peers)

        @pl.when(turn < peers)
        def _():
            push(
                MSG.at[s], RIM.at[s], bsend.at[turn - 1], brecv.at[turn - 1], beside(0, 1)
            ).wait_recv()

        high_half = quarter >= 2
        x_rows = [RIM[s, pl.ds(h, 8, stride=2), :] for h in range(2)]
        z_rows = [RIM[s, pl.ds(32 + h, 8, stride=2), :] for h in range(2)]
        y_slab = RIM[s, 16:32]
        for c in range(4):
            for facing in range(2):
                index = 16 * (2 * c + facing) + (third >> 1)
                ghost = jnp.where(
                    high_half, lane_take(x_rows[1], index), lane_take(x_rows[0], index)
                )
                for colour in range(2):
                    if c == 3:
                        PV[s, colour, facing * 17] = ghost
                    else:
                        U[s, colour, c, facing * 17] = ghost
            index = 32 * c + jnp.where((lane16 >> 5) == 3, 16, 0) + ((lane16 & 31) >> 1)
            GY[c] = lane_take(y_slab, index)

        def prepare(j, carry):
            ghost_z, ghost_y = [], []
            for c in range(4):
                index = 32 * c + j + jnp.where(z_last, 16, 0)
                ghost_z.append(
                    jnp.where(high_half, lane_take(z_rows[1], index), lane_take(z_rows[0], index))
                )
                ghost_y.append(jnp.broadcast_to(GY[c, pl.ds(j, 1), :], TILE))
            for colour in range(2):
                own_tile = PV[s, colour, j + 1]
                other = PV.at[s, 1 - colour]
                tile = other[j + 1]
                beside_it = [
                    tile,
                    far(colour, other[j], other[j + 2]),
                    jnp.where(y_first, ghost_y[3], y_down(tile)),
                    jnp.where(y_last, ghost_y[3], y_up(tile)),
                    jnp.where(z_first, ghost_z[3], pltpu.roll(tile, 1, 1)),
                    jnp.where(z_last, ghost_z[3], pltpu.roll(tile, 127, 1)),
                ]
                face = [0.5 * (own_tile + value) for value in beside_it]
                diagonal = REACTION + face[0]
                for value in face[1:]:
                    diagonal = diagonal + value
                rim_y = jnp.where(y_first, face[2], jnp.where(y_last, face[3], 0.0))
                rim_z = jnp.where(z_first, face[4], jnp.where(z_last, face[5], 0.0))
                for c in range(3):
                    LD[s, colour, c, j] = (
                        LD[s, colour, c, j] + rim_y * ghost_y[c] + rim_z * ghost_z[c]
                    )
                W[colour, j, 0] = face[0]
                W[colour, j, 1] = face[1]
                W[colour, j, 2] = jnp.where(y_first, 0.0, face[2])
                W[colour, j, 3] = jnp.where(y_last, 0.0, face[3])
                W[colour, j, 4] = jnp.where(z_first, 0.0, face[4])
                W[colour, j, 5] = jnp.where(z_last, 0.0, face[5])
                W[colour, j, 6] = diagonal
                W[colour, j, 7] = 1.0 / diagonal
            return carry

        lax.fori_loop(0, EDGE, prepare, 0)

        for sweep in range(SWEEPS):
            for colour in range(2):
                last = sweep == SWEEPS - 1 and colour == 1

                def update(j, carry, colour=colour, last=last):
                    weights = [W[colour, j, k] for k in range(8)]
                    for c in range(3):
                        summed = total(s, colour, c, j, weights)
                        new = summed * weights[7]
                        U[s, colour, c, j + 1] = new
                        if last:
                            RB[c, j] = summed - weights[6] * new
                    return carry

                lax.fori_loop(0, EDGE, update, 0)

        taken = RIM[s, 48:56]

        def finish(big, carry):
            tiles = [[], [], [], [], [], []]
            for small in range(4):
                j = 4 * big + small
                weights = [W[0, j, k] for k in range(7)]
                for c in range(3):
                    red, black = U[s, 0, c, j + 1], U[s, 1, c, j + 1]
                    left = total(s, 0, c, j, weights) - weights[6] * red
                    tiles[c].append(left + RB[c, j])
                    tiles[3 + c].append(red + black)
                    start = c * 1024 + 64 * j + s
                    fo[pl.ds(start, 8, stride=SLOTS), :] = jnp.where(even, red, black) * taken
                    fo[pl.ds(start + 32, 8, stride=SLOTS), :] = (
                        jnp.where(even, black, red) * taken
                    )
            even_z = (third & 1) == 0
            even_y = (quarter & 1) == 0
            for k in range(6):
                halves = []
                for h in range(2):
                    one, two = tiles[k][2 * h], tiles[k][2 * h + 1]
                    halves.append(
                        jnp.where(
                            even_z, one + pltpu.roll(one, 127, 1), two + pltpu.roll(two, 1, 1)
                        )
                    )
                MEAN[s, k, big] = 0.125 * jnp.where(
                    even_y,
                    halves[0] + pltpu.roll(halves[0], 96, 1),
                    halves[1] + pltpu.roll(halves[1], 32, 1),
                )
            return carry

        lax.fori_loop(0, 4, finish, 0)

        @pl.when(turn < peers)
        def _():
            push(
                MEAN.at[s], RET.at[me], csend.at[turn - 1], crecv.at[turn - 1], {"gx": s}
            ).start()

        return carry

    lax.fori_loop(1, peers + 1, one_slot, 0)
    RET[me] = MEAN[me]

    for turn in range(1, peers):
        owner_at = lax.rem(me + turn, peers)
        push(
            MEAN.at[owner_at], RET.at[owner_at], csend.at[turn - 1], crecv.at[turn - 1], beside(0, 1)
        ).wait_recv()

    first_here = (lane >> 4) == positions[0]
    second_here = (lane >> 4) == positions[1]

    def spread(big, carry):
        for k in range(6):
            first = RET[groups[0], k, big]
            second = RET[groups[1], k, big]
            for small in range(4):
                x = 4 * big + small
                for h in range(2):
                    index = (2 * h + (small >> 1)) * 32 + (small & 1) + 2 * (lane & 15)
                    rows = pl.ds(h, 8, stride=2)
                    base = C[k - 3, x + 1, rows, :] if k >= 3 else jnp.zeros(TILE, jnp.float32)
                    value = jnp.where(
                        first_here,
                        lane_take(first, index),
                        jnp.where(second_here, lane_take(second, index), base),
                    )
                    if k >= 3:
                        SP[k - 3, x + 1, rows, :] = value
                        so[k - 3, x, rows, :] = value
                    else:
                        RM[k, x, rows, :] = value
        return carry

    lax.fori_loop(0, 4, spread, 0)

    outward2 = faces(SP, pl.ds(1, EDGE), HX2, HY2, HZ2, ZF2, dsend, drecv)
    for copy in outward2[:4]:
        copy.start()
    packed = jnp.zeros(SLAB, jnp.float32)
    for c in range(3):
        for x in range(EDGE):
            plane = SP[c, x + 1]
            low, high = 32 * c + x, 32 * c + 16 + x
            packed = jnp.where(lane16 == low, pltpu.roll(plane, (low - 127) % 128, 1), packed)
            packed = jnp.where(lane16 == high, pltpu.roll(plane, high, 1), packed)
    ZF2[...] = packed
    for copy in outward2[4:]:
        copy.start()

    for facing in range(2):
        for c in range(4):
            C[c, facing * 17] = HX[facing, c]
    loads[5].wait()
    for copy in outward2:
        copy.wait_recv()
    for facing in range(2):
        outside = at[0] == (size[0] - 1 if facing else 0)
        SP[:, facing * 17] = jnp.where(outside, 0.0, HX2[facing])
        outside = at[1] == (size[1] - 1 if facing else 0)
        HY2[facing] = jnp.where(outside, 0.0, HY2[facing])
        outside = at[2] == (size[2] - 1 if facing else 0)
        HZ2[facing] = jnp.where(outside, 0.0, HZ2[facing])

    refined_here = (group16 == positions[0]) | (group16 == positions[1])

    def leftover(x, carry):
        def neighbours(block, c, hy, hz):
            centre = block[c, x + 1]
            lanes = [
                lane_take(hz[f], jnp.full(SLAB, 32 * c + 16 * f, jnp.int32) + x) for f in range(2)
            ]
            rows = [jnp.broadcast_to(hy[f, c, pl.ds(x, 1), :], SLAB) for f in range(2)]
            return centre, [
                block[c, x],
                block[c, x + 2],
                jnp.where(row16 == 0, rows[0], pltpu.roll(centre, 1, 0)),
                jnp.where(row16 == 15, rows[1], pltpu.roll(centre, 15, 0)),
                jnp.where(lane16 == 0, lanes[0], pltpu.roll(centre, 1, 1)),
                jnp.where(lane16 == 127, lanes[1], pltpu.roll(centre, 127, 1)),
            ]

        centre, near = neighbours(C, 3, HY, HZ)
        face = [0.5 * (centre + value) for value in near]
        for c in range(3):
            centre, near = neighbours(SP, c, HY2, HZ2)
            applied = face[0] * (centre - near[0])
            for k in range(1, 6):
                applied = applied + face[k] * (centre - near[k])
            left = CR[c, x] - (REACTION * centre + 0.25 * applied)
            ro[c, x] = jnp.where(refined_here, RM[c, x], left)
        return carry

    lax.fori_loop(0, EDGE, leftover, 0)

    for copy in outward + out_rims + outward2:
        copy.wait_send()
    for turn in range(1, peers):
        owner_at = lax.rem(me + turn, peers)
        push(
            MEAN.at[owner_at], RET.at[owner_at], csend.at[turn - 1], crecv.at[turn - 1], beside(0, 1)
        ).wait_send()


def shards(cv, cm, cr, fv, fr, fm, refined, owner):
    def rows_of(values):
        return values[0].transpose(1, 0, 2).reshape(3, SLOTS, 256, 128).transpose(
            0, 2, 1, 3
        ).reshape(3072, 128)

    f32 = jnp.float32
    vmem = lambda *shape: pltpu.VMEM(shape, f32)
    dma = lambda count: pltpu.SemaphoreType.DMA((count,))
    any_space = pl.BlockSpec(memory_space=pl.ANY)
    in_vmem = pl.BlockSpec(memory_space=pltpu.VMEM)
    in_smem = pl.BlockSpec(memory_space=pltpu.SMEM)
    shape = jax.ShapeDtypeStruct
    fine, synced, residual = pl.pallas_call(
        kernel,
        name="smooth",
        out_shape=[
            shape((3072, 128), f32),
            shape((3, 16, 16, 128), f32),
            shape((3, 16, 16, 128), f32),
        ],
        in_specs=[any_space] * 6 + [in_smem] * 2,
        out_specs=[in_vmem] * 3,
        scratch_shapes=[
            vmem(4, 18, 16, 128),
            vmem(3, 16, 16, 128),
            vmem(3072, 128),
            vmem(3072, 128),
            vmem(1024, 128),
            vmem(2, 4, 16, 128),
            vmem(2, 4, 16, 128),
            vmem(2, 16, 128),
            vmem(2, 4, 16, 128),
            vmem(16, 128),
            vmem(4, 56, 128),
            vmem(4, 56, 128),
            vmem(4, 2, 18, 8, 128),
            vmem(4, 2, 3, 18, 8, 128),
            vmem(4, 2, 3, 16, 8, 128),
            vmem(2, 16, 8, 8, 128),
            vmem(4, 16, 128),
            vmem(3, 16, 8, 128),
            vmem(4, 6, 4, 8, 128),
            vmem(4, 6, 4, 8, 128),
            vmem(3, 18, 16, 128),
            vmem(3, 16, 16, 128),
            vmem(2, 3, 16, 128),
            vmem(2, 3, 16, 128),
            vmem(2, 16, 128),
            vmem(16, 128),
            dma(6), dma(6), dma(6), dma(3), dma(3), dma(3), dma(3), dma(6), dma(6),
        ],
        compiler_params=pltpu.CompilerParams(
            collective_id=0, has_side_effects=True, vmem_limit_bytes=48 * 2**20
        ),
    )(
        cv, cm, cr, rows_of(fv), rows_of(fr),
        fm[0].reshape(SLOTS, 256, 128).transpose(1, 0, 2).reshape(1024, 128),
        refined, owner,
    )
    fine = fine.reshape(3, 256, SLOTS, 128).transpose(0, 2, 1, 3).reshape(3, SLOTS, 32768)
    return fine.transpose(1, 0, 2)[None], synced, residual


def solution(mesh):
    block = P(None, "gx", "gy", "gz")
    slots = P(("gx", "gy", "gz"))
    return jax.shard_map(
        shards,
        mesh=mesh,
        in_specs=(block, P("gx", "gy", "gz"), block, slots, slots, slots, slots, slots),
        out_specs=(slots, block, block),
        check_vma=False,
    )
```

time: 568 us -> 103 us (0.18); the launches traced: 557 us -> 102 us
  local copies, waits for them, and re-layouts: 385 us -> 9.28 us
  other arithmetic: 116 us -> 0 us
  Pallas kernels: 0 us -> 92.4 us
  starting transfers between devices: 50.4 us -> 0 us
    pallas_call x0 -> x1, Pallas kernels: none -> 92.4 us  [shards(): pl.pallas_call(kernel, name='smooth', out_shape=[shape((3072, 128), f32),...]
    reshape x19 -> x0, local copies, waits for them, and re-layouts: 71.4 us -> none  [the longest x6 42.4 us: ghost_field(): return jnp.pad(widened, padding).reshape(face.shape[0], 4, -1)]
    scatter x2 -> x0, local copies, waits for them, and re-layouts: 64.7 us -> none  [the longest x1 32.3 us: shards(): synced = coarse_velocity.reshape(3, -1).at[:, cell_index].set(mean_veloci...]
    reduce_sum x3 -> x0, other arithmetic: 50.4 us -> none  [the longest x1 49.4 us: smooth_patches(): averaged = 0.125 * jnp.sum(blocks, axis=(3, 5, 7))]
    slice x31 -> x0, local copies, waits for them, and re-layouts: 47.7 us -> none  [the longest x15 23 us: shifted(): return jnp.concatenate([filler, values[..., :offset]], axis=-1)]
    unnamed x92 -> x17, local copies, waits for them, and re-layouts: 52.2 us -> 9.28 us
    concatenate x3 -> x0, local copies, waits for them, and re-layouts: 39.6 us -> none  [the longest x1 30.8 us: smooth_patches(): joined = jnp.concatenate([residual, state], axis=1)]
    ppermute x12 -> x0, starting transfers between devices: 37.3 us -> none  [the longest x6 27.7 us: with_halo(): lax.ppermute(tail, axis, [(i, (i + 1) % count) for i in range(ends)])]
  transfers between devices with their start and end apart: 15 -> 0, of which waited for: 1 -> 0; matrix products, arithmetic and copies ran while one was open for 19% -> 0% of each run, Pallas kernels for 0% -> 0%
where the time goes in v1:
time: 103 us; the launch traced here: 102 us
  Pallas kernels  92.4 us (90%)
  local copies, waits for them, and re-layouts  9.28 us (9%)
    pallas_call x1, Pallas kernels, shards(): pl.pallas_call(kernel, name='smooth', out_shape=[shape((3072, 128), f32),...  92.4 us
    unnamed x17, local copies, waits for them, and re-layouts  9.28 us

profile of v1, /device:TPU:1, one launch (start us, length us, event | category | flops | bytes accessed | tf_op | source)
XLA Modules:
  0.0 102.3 jit_solution(2176688029730059786)
XLA Ops:
  0.6 0.0 copy-start
  0.6 1.4 %copy-done = f32[1,4,3,32768]{3,1,2,0:T(4,128)S(1)} copy-done((f32[1,4,3,32768]{3,1,2,0:T(4,128)S(1)}, f32[1,4,3,32768]{3,1,2,0:T(4,128)}, u32[]{:S(2)}) %copy-start) | copy-done | bytes 1572888
  2.0 0.0 copy-start.1
  2.0 1.0 %copy-done.1 = f32[1,4,32768]{2,1,0:T(4,128)S(1)} copy-done((f32[1,4,32768]{2,1,0:T(4,128)S(1)}, f32[1,4,32768]{2,1,0:T(4,128)}, u32[]{:S(2)}) %copy-start.1) | copy-done | bytes 524312
  3.1 0.0 copy-start.2
  3.1 1.0 copy-done.2
  4.1 0.0 copy-start.3
  4.1 1.0 copy-done.3
  5.1 0.0 copy-start.4
  5.1 0.9 copy-done.4
  6.0 0.0 copy-start.5
  6.0 0.7 copy-done.5
  6.6 0.0 copy-start.6
  6.6 0.7 copy-done.6
  7.3 92.4 %smooth.1 = (f32[3072,128]{1,0:T(8,128)S(1)}, f32[3,16,16,128]{3,2,1,0:T(8,128)S(1)}, f32[3,16,16,128]{3,2,1,0:T(8,128)S(1)}) custom-call(f32[3,16,16,128]{3,2,1,0:T(8,128)S(1)} %copy-done.2, f32[16,16,128]{2,1,0:T(8,128)S(1)} %copy-done.4, f32[3,16,16,128]{3,2,1,0:T(8,128)S(1)} %copy-done.3, f32[3072,128]{1,0:T(8,128)S(1)} %bitcast.32, ...), custom_call_target="tpu_custom_call" | custom-call | tf_op jit(solution)/shard_map/smooth/pallas_call | solution.py:471
  99.7 1.1 %copy.17 = f32[1,4,3,32768]{3,1,2,0:T(4,128)} copy(f32[1,4,3,32768]{3,1,2,0:T(4,128)S(1)} %bitcast.33) | data formatting | bytes 3145728
  100.8 0.7 copy.18
  101.6 0.7 copy.19
Async XLA Ops:
  0.6 1.4 %copy-start = (f32[1,4,3,32768]{3,1,2,0:T(4,128)S(1)}, f32[1,4,3,32768]{3,1,2,0:T(4,128)}, u32[]{:S(2)}) copy-start(f32[1,4,3,32768]{3,1,2,0:T(4,128)} %param.11) | copy-start | bytes 4718596
  2.0 1.0 %copy-start.1 = (f32[1,4,32768]{2,1,0:T(4,128)S(1)}, f32[1,4,32768]{2,1,0:T(4,128)}, u32[]{:S(2)}) copy-start(f32[1,4,32768]{2,1,0:T(4,128)} %param.13) | copy-start | bytes 1572868
  3.1 1.0 copy-start.2
  4.1 1.0 copy-start.3
  5.1 0.9 copy-start.4
  6.0 0.7 copy-start.5
  6.6 0.7 copy-start.6

commit v2 on v1

--- a/solution.py
+++ b/solution.py
@@ -10,6 +10,7 @@
 SWEEPS = 2
 EDGE = 16
 SLOTS = 4
+GROUP = 16
 REACTION = 1.0
 TILE = (8, 128)
 SLAB = (16, 128)
@@ -46,10 +47,10 @@
 
 
 def kernel(
-    cv, cm, cr, fv, fr, fm, place, own,
-    fo, so, ro,
-    C, CR, FV, FR, FM, HX, HY, HZ, EF, ZF, MSG, RIM, PV, U, LD, W, GY, RB,
-    MEAN, RET, SP, RM, HX2, HY2, HZ2, ZF2,
+    cv, cm, cr, fv, fr, fm, place_in, own_in,
+    fo, C, CR, HY, HZ, SP, RM, HY2, HZ2, mask,
+    FV, FR, FM, HX, EF, ZF, MSG, RIM, PV, U, LD, W, GY, RB,
+    MEAN, RET, HX2, ZF2, place, own,
     lsem, asend, arecv, bsend, brecv, csend, crecv, dsend, drecv,
 ):
     at = [lax.axis_index(axis) for axis in AXES]
@@ -66,6 +67,8 @@
         pltpu.make_async_copy(fr, FR, lsem.at[3]),
         pltpu.make_async_copy(fv, FV, lsem.at[4]),
         pltpu.make_async_copy(cr, CR, lsem.at[5]),
+        pltpu.make_async_copy(place_in, place, lsem.at[6]),
+        pltpu.make_async_copy(own_in, own, lsem.at[7]),
     ]
     for load in loads:
         load.start()
@@ -78,8 +81,6 @@
             pl.semaphore_signal(
                 barrier, inc=1, device_id=beside(number, step), device_id_type=MESH
             )
-    pl.semaphore_wait(barrier, peers + 3)
-
     lane = lax.broadcasted_iota(jnp.int32, TILE, 1)
     row = lax.broadcasted_iota(jnp.int32, TILE, 0)
     third = lane & 31
@@ -92,8 +93,6 @@
     row16 = lax.broadcasted_iota(jnp.int32, SLAB, 0)
     group16 = lane16 >> 4
     inner16 = lane16 & 15
-    positions = [place[0, 0], place[0, 1]]
-    groups = [lax.div(own[0, i], size[1] * size[2]) for i in range(2)]
 
     def faces(block, planes, hx, hy, hz, packed, sent, landed):
         first, last = 1, EDGE
@@ -108,9 +107,6 @@
 
     loads[0].wait()
     loads[1].wait()
-    outward = faces(C, pl.ds(1, EDGE), HX, HY, HZ, ZF, asend, arecv)
-    for copy in outward[:4]:
-        copy.start()
     packed = jnp.zeros(SLAB, jnp.float32)
     for c in range(4):
         upper = jnp.zeros(SLAB, jnp.float32)
@@ -126,7 +122,9 @@
         packed = jnp.where(group16 == 2 * c, pltpu.roll(upper, turn, 1), packed)
         packed = jnp.where(group16 == 2 * c + 1, pltpu.roll(lower, turn, 1), packed)
     ZF[...] = packed
-    for copy in outward[4:]:
+    pl.semaphore_wait(barrier, peers + 3)
+    outward = faces(C, pl.ds(1, EDGE), HX, HY, HZ, ZF, asend, arecv)
+    for copy in outward:
         copy.start()
 
     loads[2].wait()
@@ -146,7 +144,58 @@
                 U[s, 0, c, j + 1], U[s, 1, c, j + 1] = pair(FV, c * 1024 + s)
         return carry
 
+    def y_up(tile):
+        turned = pltpu.roll(tile, 96, 1)
+        return jnp.where(quarter == 3, pltpu.roll(turned, 7, 0), turned)
+
+    def y_down(tile):
+        turned = pltpu.roll(tile, 32, 1)
+        return jnp.where(quarter == 0, pltpu.roll(turned, 1, 0), turned)
+
+    def far(colour, before, after):
+        if colour == 0:
+            return jnp.where(even, before, after)
+        return jnp.where(even, after, before)
+
+    def prepare(step, carry):
+        s, big = step >> 2, step & 3
+        stores = []
+        for small in range(4):
+            j = 4 * big + small
+            for colour in range(2):
+                own_tile = PV[s, colour, j + 1]
+                other = PV.at[s, 1 - colour]
+                tile = other[j + 1]
+                face = [
+                    0.5 * (own_tile + value)
+                    for value in (
+                        tile,
+                        far(colour, other[j], other[j + 2]),
+                        jnp.where(y_first, 0.0, y_down(tile)),
+                        jnp.where(y_last, 0.0, y_up(tile)),
+                        jnp.where(z_first, 0.0, pltpu.roll(tile, 1, 1)),
+                        jnp.where(z_last, 0.0, pltpu.roll(tile, 127, 1)),
+                    )
+                ]
+                diagonal = REACTION + face[0]
+                for value in face[1:]:
+                    diagonal = diagonal + value
+                inside = face[:2] + [
+                    jnp.where(outer, 0.0, value)
+                    for outer, value in zip((y_first, y_last, z_first, z_last), face[2:])
+                ]
+                stores.append((colour, j, inside + [diagonal]))
+        for colour, j, values in stores:
+            for k, value in enumerate(values):
+                W[s, colour, j, k] = value
+        return carry
+
+    for s in range(SLOTS):
+        for colour in range(2):
+            for end in (0, EDGE + 1):
+                PV[s, colour, end] = jnp.zeros(TILE, jnp.float32)
     lax.fori_loop(0, EDGE, pack, 0)
+    lax.fori_loop(0, EDGE, prepare, 0)
 
     for copy in outward:
         copy.wait_recv()
@@ -158,6 +207,10 @@
         outside = at[2] == (size[2] - 1 if facing else 0)
         HZ[facing] = jnp.where(outside, 0.0, HZ[facing])
 
+    loads[6].wait()
+    loads[7].wait()
+    positions = [place[0, 0], place[0, 1]]
+    groups = [lax.div(own[0, i], size[1] * size[2]) for i in range(2)]
     odd_group = (group16 & 1) == 1
     across = jnp.where(odd_group, HZ[1], HZ[0])
     rims = []
@@ -195,19 +248,6 @@
         out_rims[-1].start()
     RIM[me] = MSG[me]
 
-    def y_up(tile):
-        turned = pltpu.roll(tile, 96, 1)
-        return jnp.where(quarter == 3, pltpu.roll(turned, 7, 0), turned)
-
-    def y_down(tile):
-        turned = pltpu.roll(tile, 32, 1)
-        return jnp.where(quarter == 0, pltpu.roll(turned, 1, 0), turned)
-
-    def far(colour, before, after):
-        if colour == 0:
-            return jnp.where(even, before, after)
-        return jnp.where(even, after, before)
-
     def total(s, colour, c, j, weights):
         other = U.at[s, 1 - colour, c]
         tile = other[j + 1]
@@ -234,97 +274,109 @@
         x_rows = [RIM[s, pl.ds(h, 8, stride=2), :] for h in range(2)]
         z_rows = [RIM[s, pl.ds(32 + h, 8, stride=2), :] for h in range(2)]
         y_slab = RIM[s, 16:32]
+        rim_x = []
         for c in range(4):
             for facing in range(2):
                 index = 16 * (2 * c + facing) + (third >> 1)
                 ghost = jnp.where(
                     high_half, lane_take(x_rows[1], index), lane_take(x_rows[0], index)
                 )
-                for colour in range(2):
-                    if c == 3:
-                        PV[s, colour, facing * 17] = ghost
-                    else:
+                if c == 3:
+                    rim_x.append(ghost)
+                else:
+                    for colour in range(2):
                         U[s, colour, c, facing * 17] = ghost
             index = 32 * c + jnp.where((lane16 >> 5) == 3, 16, 0) + ((lane16 & 31) >> 1)
             GY[c] = lane_take(y_slab, index)
-
-        def prepare(j, carry):
-            ghost_z, ghost_y = [], []
-            for c in range(4):
-                index = 32 * c + j + jnp.where(z_last, 16, 0)
-                ghost_z.append(
-                    jnp.where(high_half, lane_take(z_rows[1], index), lane_take(z_rows[0], index))
-                )
-                ghost_y.append(jnp.broadcast_to(GY[c, pl.ds(j, 1), :], TILE))
-            for colour in range(2):
-                own_tile = PV[s, colour, j + 1]
-                other = PV.at[s, 1 - colour]
-                tile = other[j + 1]
-                beside_it = [
-                    tile,
-                    far(colour, other[j], other[j + 2]),
-                    jnp.where(y_first, ghost_y[3], y_down(tile)),
-                    jnp.where(y_last, ghost_y[3], y_up(tile)),
-                    jnp.where(z_first, ghost_z[3], pltpu.roll(tile, 1, 1)),
-                    jnp.where(z_last, ghost_z[3], pltpu.roll(tile, 127, 1)),
-                ]
-                face = [0.5 * (own_tile + value) for value in beside_it]
-                diagonal = REACTION + face[0]
-                for value in face[1:]:
-                    diagonal = diagonal + value
-                rim_y = jnp.where(y_first, face[2], jnp.where(y_last, face[3], 0.0))
-                rim_z = jnp.where(z_first, face[4], jnp.where(z_last, face[5], 0.0))
+        for colour in range(2):
+            for facing in range(2):
+                j = (EDGE - 1) * facing
+                at_rim = even if colour == facing else jnp.logical_not(even)
+                more = jnp.where(at_rim, 0.5 * rim_x[facing], 0.0)
+                W[s, colour, j, 1] = W[s, colour, j, 1] + more
+                W[s, colour, j, 6] = W[s, colour, j, 6] + more
+
+        at_z = z_first | z_last
+        at_y = y_first | y_last
+
+        def surround(big, carry):
+            stores = []
+            for small in range(4):
+                j = 4 * big + small
+                ghost_z, ghost_y = [], []
+                for c in range(4):
+                    index = 32 * c + j + jnp.where(z_last, 16, 0)
+                    ghost_z.append(
+                        jnp.where(
+                            high_half, lane_take(z_rows[1], index), lane_take(z_rows[0], index)
+                        )
+                    )
+                    ghost_y.append(jnp.broadcast_to(GY[c, pl.ds(j, 1), :], TILE))
+                for colour in range(2):
+                    half = 0.5 * PV[s, colour, j + 1]
+                    half_z, half_y = 0.5 * ghost_z[3], 0.5 * ghost_y[3]
+                    rim_z = jnp.where(at_z, half + half_z, 0.0)
+                    rim_y = jnp.where(at_y, half + half_y, 0.0)
+                    diagonal = (
+                        W[s, colour, j, 6]
+                        + jnp.where(at_z, half_z, 0.0)
+                        + jnp.where(at_y, half_y, 0.0)
+                    )
+                    loaded = [
+                        LD[s, colour, c, j] + rim_y * ghost_y[c] + rim_z * ghost_z[c]
+                        for c in range(3)
+                    ]
+                    stores.append((colour, j, diagonal, 1.0 / diagonal, loaded))
+            for colour, j, diagonal, inverse, loaded in stores:
+                W[s, colour, j, 6] = diagonal
+                W[s, colour, j, 7] = inverse
                 for c in range(3):
-                    LD[s, colour, c, j] = (
-                        LD[s, colour, c, j] + rim_y * ghost_y[c] + rim_z * ghost_z[c]
-                    )
-                W[colour, j, 0] = face[0]
-                W[colour, j, 1] = face[1]
-                W[colour, j, 2] = jnp.where(y_first, 0.0, face[2])
-                W[colour, j, 3] = jnp.where(y_last, 0.0, face[3])
-                W[colour, j, 4] = jnp.where(z_first, 0.0, face[4])
-                W[colour, j, 5] = jnp.where(z_last, 0.0, face[5])
-                W[colour, j, 6] = diagonal
-                W[colour, j, 7] = 1.0 / diagonal
+                    LD[s, colour, c, j] = loaded[c]
             return carry
 
-        lax.fori_loop(0, EDGE, prepare, 0)
+        lax.fori_loop(0, 4, surround, 0)
 
         for sweep in range(SWEEPS):
             for colour in range(2):
                 last = sweep == SWEEPS - 1 and colour == 1
 
-                def update(j, carry, colour=colour, last=last):
-                    weights = [W[colour, j, k] for k in range(8)]
-                    for c in range(3):
-                        summed = total(s, colour, c, j, weights)
-                        new = summed * weights[7]
+                def update(big, carry, colour=colour, last=last):
+                    stores = []
+                    for small in range(GROUP):
+                        j = GROUP * big + small
+                        weights = [W[s, colour, j, k] for k in range(8)]
+                        for c in range(3):
+                            summed = total(s, colour, c, j, weights)
+                            new = summed * weights[7]
+                            left = summed - weights[6] * new if last else None
+                            stores.append((c, j, new, left))
+                    for c, j, new, left in stores:
                         U[s, colour, c, j + 1] = new
                         if last:
-                            RB[c, j] = summed - weights[6] * new
+                            RB[c, j] = left
                     return carry
 
-                lax.fori_loop(0, EDGE, update, 0)
+                lax.fori_loop(0, EDGE // GROUP, update, 0)
 
         taken = RIM[s, 48:56]
 
         def finish(big, carry):
             tiles = [[], [], [], [], [], []]
+            stores = []
             for small in range(4):
                 j = 4 * big + small
-                weights = [W[0, j, k] for k in range(7)]
+                weights = [W[s, 0, j, k] for k in range(7)]
                 for c in range(3):
                     red, black = U[s, 0, c, j + 1], U[s, 1, c, j + 1]
                     left = total(s, 0, c, j, weights) - weights[6] * red
                     tiles[c].append(left + RB[c, j])
                     tiles[3 + c].append(red + black)
                     start = c * 1024 + 64 * j + s
-                    fo[pl.ds(start, 8, stride=SLOTS), :] = jnp.where(even, red, black) * taken
-                    fo[pl.ds(start + 32, 8, stride=SLOTS), :] = (
-                        jnp.where(even, black, red) * taken
-                    )
+                    stores.append((start, jnp.where(even, red, black) * taken))
+                    stores.append((start + 32, jnp.where(even, black, red) * taken))
             even_z = (third & 1) == 0
             even_y = (quarter & 1) == 0
+            means = []
             for k in range(6):
                 halves = []
                 for h in range(2):
@@ -334,11 +386,18 @@
                             even_z, one + pltpu.roll(one, 127, 1), two + pltpu.roll(two, 1, 1)
                         )
                     )
-                MEAN[s, k, big] = 0.125 * jnp.where(
-                    even_y,
-                    halves[0] + pltpu.roll(halves[0], 96, 1),
-                    halves[1] + pltpu.roll(halves[1], 32, 1),
+                means.append(
+                    0.125
+                    * jnp.where(
+                        even_y,
+                        halves[0] + pltpu.roll(halves[0], 96, 1),
+                        halves[1] + pltpu.roll(halves[1], 32, 1),
+                    )
                 )
+            for k in range(6):
+                MEAN[s, k, big] = means[k]
+            for start, tile in stores:
+                fo[pl.ds(start, 8, stride=SLOTS), :] = tile
             return carry
 
         lax.fori_loop(0, 4, finish, 0)
@@ -364,6 +423,7 @@
     second_here = (lane >> 4) == positions[1]
 
     def spread(big, carry):
+        stores = []
         for k in range(6):
             first = RET[groups[0], k, big]
             second = RET[groups[1], k, big]
@@ -378,11 +438,12 @@
                         lane_take(first, index),
                         jnp.where(second_here, lane_take(second, index), base),
                     )
-                    if k >= 3:
-                        SP[k - 3, x + 1, rows, :] = value
-                        so[k - 3, x, rows, :] = value
-                    else:
-                        RM[k, x, rows, :] = value
+                    stores.append((k, x, rows, value))
+        for k, x, rows, value in stores:
+            if k >= 3:
+                SP[k - 3, x + 1, rows, :] = value
+            else:
+                RM[k, x, rows, :] = value
         return carry
 
     lax.fori_loop(0, 4, spread, 0)
@@ -416,9 +477,32 @@
         HZ2[facing] = jnp.where(outside, 0.0, HZ2[facing])
 
     refined_here = (group16 == positions[0]) | (group16 == positions[1])
-
-    def leftover(x, carry):
-        def neighbours(block, c, hy, hz):
+    mask[...] = jnp.where(refined_here, 1.0, 0.0)
+    for copy in outward + out_rims + outward2:
+        copy.wait_send()
+    for turn in range(1, peers):
+        owner_at = lax.rem(me + turn, peers)
+        push(
+            MEAN.at[owner_at], RET.at[owner_at], csend.at[turn - 1], crecv.at[turn - 1], beside(0, 1)
+        ).wait_send()
+
+
+def write_out(
+    fine, C, CR, HY, HZ, SP, RM, HY2, HZ2, mask, fo, so, ro, R, sem
+):
+    copies = [
+        pltpu.make_async_copy(SP.at[:, 1 : EDGE + 1], so, sem.at[0]),
+        pltpu.make_async_copy(fine, fo, sem.at[1]),
+        pltpu.make_async_copy(R, ro, sem.at[2]),
+    ]
+    copies[0].start()
+    copies[1].start()
+    lane16 = lax.broadcasted_iota(jnp.int32, SLAB, 1)
+    row16 = lax.broadcasted_iota(jnp.int32, SLAB, 0)
+    refined_here = mask[...] > 0.5
+
+    def leftover(big, carry):
+        def neighbours(block, c, x, hy, hz):
             centre = block[c, x + 1]
             lanes = [
                 lane_take(hz[f], jnp.full(SLAB, 32 * c + 16 * f, jnp.int32) + x) for f in range(2)
@@ -433,26 +517,26 @@
                 jnp.where(lane16 == 127, lanes[1], pltpu.roll(centre, 127, 1)),
             ]
 
-        centre, near = neighbours(C, 3, HY, HZ)
-        face = [0.5 * (centre + value) for value in near]
-        for c in range(3):
-            centre, near = neighbours(SP, c, HY2, HZ2)
-            applied = face[0] * (centre - near[0])
-            for k in range(1, 6):
-                applied = applied + face[k] * (centre - near[k])
-            left = CR[c, x] - (REACTION * centre + 0.25 * applied)
-            ro[c, x] = jnp.where(refined_here, RM[c, x], left)
+        stores = []
+        for small in range(2):
+            x = 2 * big + small
+            centre, near = neighbours(C, 3, x, HY, HZ)
+            face = [0.5 * (centre + value) for value in near]
+            for c in range(3):
+                centre, near = neighbours(SP, c, x, HY2, HZ2)
+                applied = face[0] * (centre - near[0])
+                for k in range(1, 6):
+                    applied = applied + face[k] * (centre - near[k])
+                left = CR[c, x] - (REACTION * centre + 0.25 * applied)
+                stores.append((c, x, jnp.where(refined_here, RM[c, x], left)))
+        for c, x, left in stores:
+            R[c, x] = left
         return carry
 
-    lax.fori_loop(0, EDGE, leftover, 0)
-
-    for copy in outward + out_rims + outward2:
-        copy.wait_send()
-    for turn in range(1, peers):
-        owner_at = lax.rem(me + turn, peers)
-        push(
-            MEAN.at[owner_at], RET.at[owner_at], csend.at[turn - 1], crecv.at[turn - 1], beside(0, 1)
-        ).wait_send()
+    lax.fori_loop(0, EDGE // 2, leftover, 0)
+    copies[2].start()
+    for copy in copies:
+        copy.wait()
 
 
 def shards(cv, cm, cr, fv, fr, fm, refined, owner):
@@ -464,29 +548,33 @@
     f32 = jnp.float32
     vmem = lambda *shape: pltpu.VMEM(shape, f32)
     dma = lambda count: pltpu.SemaphoreType.DMA((count,))
-    any_space = pl.BlockSpec(memory_space=pl.ANY)
+    any_space = pl.BlockSpec(memory_space=pltpu.HBM)
     in_vmem = pl.BlockSpec(memory_space=pltpu.VMEM)
-    in_smem = pl.BlockSpec(memory_space=pltpu.SMEM)
     shape = jax.ShapeDtypeStruct
-    fine, synced, residual = pl.pallas_call(
+    here = lambda x: pltpu.with_memory_space_constraint(x, pltpu.HBM)
+    kept = [
+        (3072, 128),
+        (4, 18, 16, 128),
+        (3, 16, 16, 128),
+        (2, 4, 16, 128),
+        (2, 16, 128),
+        (3, 18, 16, 128),
+        (3, 16, 16, 128),
+        (2, 3, 16, 128),
+        (2, 16, 128),
+        (16, 128),
+    ]
+    held = pl.pallas_call(
         kernel,
         name="smooth",
-        out_shape=[
-            shape((3072, 128), f32),
-            shape((3, 16, 16, 128), f32),
-            shape((3, 16, 16, 128), f32),
-        ],
-        in_specs=[any_space] * 6 + [in_smem] * 2,
-        out_specs=[in_vmem] * 3,
+        out_shape=[vmem(*dims) for dims in kept],
+        in_specs=[any_space] * 8,
+        out_specs=[in_vmem] * len(kept),
         scratch_shapes=[
-            vmem(4, 18, 16, 128),
-            vmem(3, 16, 16, 128),
             vmem(3072, 128),
             vmem(3072, 128),
             vmem(1024, 128),
             vmem(2, 4, 16, 128),
-            vmem(2, 4, 16, 128),
-            vmem(2, 16, 128),
             vmem(2, 4, 16, 128),
             vmem(16, 128),
             vmem(4, 56, 128),
@@ -494,27 +582,37 @@
             vmem(4, 2, 18, 8, 128),
             vmem(4, 2, 3, 18, 8, 128),
             vmem(4, 2, 3, 16, 8, 128),
-            vmem(2, 16, 8, 8, 128),
+            vmem(4, 2, 16, 8, 8, 128),
             vmem(4, 16, 128),
             vmem(3, 16, 8, 128),
             vmem(4, 6, 4, 8, 128),
             vmem(4, 6, 4, 8, 128),
-            vmem(3, 18, 16, 128),
-            vmem(3, 16, 16, 128),
             vmem(2, 3, 16, 128),
-            vmem(2, 3, 16, 128),
-            vmem(2, 16, 128),
             vmem(16, 128),
-            dma(6), dma(6), dma(6), dma(3), dma(3), dma(3), dma(3), dma(6), dma(6),
+            pltpu.SMEM((1, 2), jnp.int32),
+            pltpu.SMEM((1, 2), jnp.int32),
+            dma(8), dma(6), dma(6), dma(3), dma(3), dma(3), dma(3), dma(6), dma(6),
         ],
         compiler_params=pltpu.CompilerParams(
             collective_id=0, has_side_effects=True, vmem_limit_bytes=48 * 2**20
         ),
     )(
-        cv, cm, cr, rows_of(fv), rows_of(fr),
-        fm[0].reshape(SLOTS, 256, 128).transpose(1, 0, 2).reshape(1024, 128),
-        refined, owner,
+        here(cv), here(cm), here(cr), here(rows_of(fv)), here(rows_of(fr)),
+        here(fm[0].reshape(SLOTS, 256, 128).transpose(1, 0, 2).reshape(1024, 128)),
+        here(refined), here(owner),
     )
+    fine, synced, residual = pl.pallas_call(
+        write_out,
+        name="write_out",
+        out_shape=[
+            shape((3072, 128), f32),
+            shape((3, 16, 16, 128), f32),
+            shape((3, 16, 16, 128), f32),
+        ],
+        in_specs=[in_vmem] * len(kept),
+        out_specs=[any_space] * 3,
+        scratch_shapes=[vmem(3, 16, 16, 128), dma(3)],
+    )(*(pltpu.with_memory_space_constraint(x, pltpu.VMEM) for x in held))
     fine = fine.reshape(3, 256, SLOTS, 128).transpose(0, 2, 1, 3).reshape(3, SLOTS, 32768)
     return fine.transpose(1, 0, 2)[None], synced, residual
 

time: 103 us -> 32.7 us (0.32)
  Pallas kernels: 92.4 us -> 31.9 us
  local copies, waits for them, and re-layouts: 9.28 us -> 0 us
    pallas_call x1 -> x2, Pallas kernels: 92.4 us -> 31.9 us  [the longest x1 29.6 us: shards(): pl.pallas_call(kernel, name='smooth', out_shape=[vmem(*dims) for dims in...]
    unnamed x17 -> x0, local copies, waits for them, and re-layouts: 9.28 us -> none
where the time goes in v2:
time: 32.7 us; the launch traced here: 32.6 us
  Pallas kernels  31.9 us (98%)
  between operations  0.64 us (2%)
    pallas_call x1, Pallas kernels, shards(): pl.pallas_call(kernel, name='smooth', out_shape=[vmem(*dims) for dims in...  29.6 us
    pallas_call x1, Pallas kernels, shards(): pl.pallas_call(write_out, name='write_out', out_shape=[shape((3072, 128),...  2.33 us

profile of v2, /device:TPU:1, one launch (start us, length us, event | category | flops | bytes accessed | tf_op | source)
XLA Modules:
  0.0 32.6 jit_solution(9555978449932656268)
XLA Ops:
  0.6 29.6 %smooth.1 = (f32[3072,128]{1,0:T(8,128)S(1)}, f32[4,18,16,128]{3,2,1,0:T(8,128)S(1)}, f32[3,16,16,128]{3,2,1,0:T(8,128)S(1)}, f32[2,4,16,128]{3,2,1,0:T(8,128)S(...) custom-call(f32[3,16,16,128]{3,2,1,0:T(8,128)} %cv.1, ...), custom_call_target="tpu_custom_call" | custom-call | tf_op jit(solution)/shard_map/smooth/pallas_call | solution.py:567
  30.2 2.3 %write_out.1 = (f32[3072,128]{1,0:T(8,128)}, f32[3,16,16,128]{3,2,1,0:T(8,128)}, f32[3,16,16,128]{3,2,1,0:T(8,128)}) custom-call(f32[3072,128]{1,0:T(8,128)S(1)} %get-tuple-element.16.fine, f32[4,18,16,128]{3,2,1,0:T(8,128)S(1)} %get-tuple-element.17.C, f32[3,16,16,128]{3,2,1,0:T(8,128)S(1)} %get-tuple-element.18.CR, ...), custom_call_target="tpu_custom_call" | custom-call | tf_op jit(solution)/shard_map/write_out/pallas_call | solution.py:604

commit v3 on v2

--- a/solution.py
+++ b/solution.py
@@ -10,7 +10,6 @@
 SWEEPS = 2
 EDGE = 16
 SLOTS = 4
-GROUP = 16
 REACTION = 1.0
 TILE = (8, 128)
 SLAB = (16, 128)
@@ -48,9 +47,9 @@
 
 def kernel(
     cv, cm, cr, fv, fr, fm, place_in, own_in,
-    fo, C, CR, HY, HZ, SP, RM, HY2, HZ2, mask,
-    FV, FR, FM, HX, EF, ZF, MSG, RIM, PV, U, LD, W, GY, RB,
-    MEAN, RET, HX2, ZF2, place, own,
+    fo, C, CR, HX, HY, HZ, RX, RY, RZ, RS, M,
+    FV, FR, FM, EF, ZF, MSG, RIM, PV, U, LD, W, GY, RB,
+    MEAN, RET, ZM, place, own,
     lsem, asend, arecv, bsend, brecv, csend, crecv, dsend, drecv,
 ):
     at = [lax.axis_index(axis) for axis in AXES]
@@ -70,8 +69,8 @@
         pltpu.make_async_copy(place_in, place, lsem.at[6]),
         pltpu.make_async_copy(own_in, own, lsem.at[7]),
     ]
-    for load in loads:
-        load.start()
+    for number in (6, 7, 0, 1, 2, 3, 4, 5):
+        loads[number].start()
 
     barrier = pltpu.get_barrier_semaphore()
     for step in range(1, peers):
@@ -94,16 +93,24 @@
     group16 = lane16 >> 4
     inner16 = lane16 & 15
 
-    def faces(block, planes, hx, hy, hz, packed, sent, landed):
-        first, last = 1, EDGE
-        return [
-            push(block.at[:, last], hx.at[0], sent.at[0], landed.at[0], beside(0, 1)),
-            push(block.at[:, first], hx.at[1], sent.at[1], landed.at[1], beside(0, -1)),
-            push(block.at[:, planes, EDGE - 1], hy.at[0], sent.at[2], landed.at[2], beside(1, 1)),
-            push(block.at[:, planes, 0], hy.at[1], sent.at[3], landed.at[3], beside(1, -1)),
-            push(packed, hz.at[0], sent.at[4], landed.at[4], beside(2, 1)),
-            push(packed, hz.at[1], sent.at[5], landed.at[5], beside(2, -1)),
-        ]
+    loads[6].wait()
+    loads[7].wait()
+    positions = [place[0, 0], place[0, 1]]
+    groups = [lax.div(own[0, i], size[1] * size[2]) for i in range(2)]
+    marks = [(groups[i] + 1).astype(jnp.float32) for i in range(2)]
+
+    def marked(numbers, wanted):
+        return jnp.where(
+            numbers[0] == wanted, marks[0], jnp.where(numbers[1] == wanted, marks[1], 0.0)
+        )
+
+    spots = [jnp.full(SLAB, positions[i], jnp.int32) for i in range(2)]
+    mark = marked(spots, group16)
+    for x in range(EDGE):
+        C[4, x + 1] = mark
+    ZF[16:32] = jnp.where((group16 & 1) == 1, marked(spots, 0), marked(spots, 7))
+    for i in range(2):
+        M[i] = jnp.where(group16 == positions[i], 1.0, 0.0)
 
     loads[0].wait()
     loads[1].wait()
@@ -121,9 +128,17 @@
         turn = (32 * c + 16) % 128
         packed = jnp.where(group16 == 2 * c, pltpu.roll(upper, turn, 1), packed)
         packed = jnp.where(group16 == 2 * c + 1, pltpu.roll(lower, turn, 1), packed)
-    ZF[...] = packed
+    ZF[0:16] = packed
     pl.semaphore_wait(barrier, peers + 3)
-    outward = faces(C, pl.ds(1, EDGE), HX, HY, HZ, ZF, asend, arecv)
+    inner = pl.ds(1, EDGE)
+    outward = [
+        push(C.at[:, EDGE], HX.at[0], asend.at[0], arecv.at[0], beside(0, 1)),
+        push(C.at[:, 1], HX.at[1], asend.at[1], arecv.at[1], beside(0, -1)),
+        push(C.at[:, inner, EDGE - 1], HY.at[0], asend.at[2], arecv.at[2], beside(1, 1)),
+        push(C.at[:, inner, 0], HY.at[1], asend.at[3], arecv.at[3], beside(1, -1)),
+        push(ZF, HZ.at[0], asend.at[4], arecv.at[4], beside(2, 1)),
+        push(ZF, HZ.at[1], asend.at[5], arecv.at[5], beside(2, -1)),
+    ]
     for copy in outward:
         copy.start()
 
@@ -138,10 +153,11 @@
             return jnp.where(even, low, high), jnp.where(even, high, low)
 
         for s in range(SLOTS):
-            PV[s, 0, j + 1], PV[s, 1, j + 1] = pair(FM, s)
+            slot = lax.rem(me + (peers - s), peers)
+            PV[s, 0, j + 1], PV[s, 1, j + 1] = pair(FM, slot)
             for c in range(3):
-                LD[s, 0, c, j], LD[s, 1, c, j] = pair(FR, c * 1024 + s)
-                U[s, 0, c, j + 1], U[s, 1, c, j + 1] = pair(FV, c * 1024 + s)
+                LD[s, 0, c, j], LD[s, 1, c, j] = pair(FR, c * 1024 + slot)
+                U[s, 0, c, j + 1], U[s, 1, c, j + 1] = pair(FV, c * 1024 + slot)
         return carry
 
     def y_up(tile):
@@ -207,12 +223,8 @@
         outside = at[2] == (size[2] - 1 if facing else 0)
         HZ[facing] = jnp.where(outside, 0.0, HZ[facing])
 
-    loads[6].wait()
-    loads[7].wait()
-    positions = [place[0, 0], place[0, 1]]
-    groups = [lax.div(own[0, i], size[1] * size[2]) for i in range(2)]
     odd_group = (group16 & 1) == 1
-    across = jnp.where(odd_group, HZ[1], HZ[0])
+    across = jnp.where(odd_group, HZ[1, 0:16], HZ[0, 0:16])
     rims = []
     for i in range(2):
         p = positions[i]
@@ -242,11 +254,11 @@
         peer = lax.rem(me + step, peers)
         out_rims.append(
             push(
-                MSG.at[peer], RIM.at[me], bsend.at[step - 1], brecv.at[step - 1], beside(0, step)
+                MSG.at[peer], RIM.at[step], bsend.at[step - 1], brecv.at[step - 1], beside(0, step)
             )
         )
         out_rims[-1].start()
-    RIM[me] = MSG[me]
+    RIM[0] = MSG[me]
 
     def total(s, colour, c, j, weights):
         other = U.at[s, 1 - colour, c]
@@ -261,13 +273,11 @@
             + weights[5] * pltpu.roll(tile, 127, 1)
         )
 
-    def one_slot(turn, carry):
-        s = lax.rem(me + (2 * peers - turn), peers)
-
-        @pl.when(turn < peers)
-        def _():
+    def one_slot(turn):
+        s = turn
+        if turn > 0:
             push(
-                MSG.at[s], RIM.at[s], bsend.at[turn - 1], brecv.at[turn - 1], beside(0, 1)
+                MSG.at[0], RIM.at[turn], bsend.at[turn - 1], brecv.at[turn - 1], beside(0, 1)
             ).wait_recv()
 
         high_half = quarter >= 2
@@ -299,10 +309,10 @@
         at_z = z_first | z_last
         at_y = y_first | y_last
 
-        def surround(big, carry):
+        def surround(big):
             stores = []
-            for small in range(4):
-                j = 4 * big + small
+            for small in range(8):
+                j = 8 * big + small
                 ghost_z, ghost_y = [], []
                 for c in range(4):
                     index = 32 * c + j + jnp.where(z_last, 16, 0)
@@ -311,7 +321,7 @@
                             high_half, lane_take(z_rows[1], index), lane_take(z_rows[0], index)
                         )
                     )
-                    ghost_y.append(jnp.broadcast_to(GY[c, pl.ds(j, 1), :], TILE))
+                    ghost_y.append(jnp.broadcast_to(GY[c, j : j + 1, :], TILE))
                 for colour in range(2):
                     half = 0.5 * PV[s, colour, j + 1]
                     half_z, half_y = 0.5 * ghost_z[3], 0.5 * ghost_y[3]
@@ -332,182 +342,235 @@
                 W[s, colour, j, 7] = inverse
                 for c in range(3):
                     LD[s, colour, c, j] = loaded[c]
+
+        for big in range(2):
+            surround(big)
+
+        def sweep(number, carry):
+            for colour in range(2):
+                stores = []
+                for j in range(EDGE):
+                    weights = [W[s, colour, j, k] for k in range(8)]
+                    for c in range(3):
+                        summed = total(s, colour, c, j, weights)
+                        new = summed * weights[7]
+                        left = summed - weights[6] * new if colour == 1 else None
+                        stores.append((c, j, new, left))
+                for c, j, new, left in stores:
+                    U[s, colour, c, j + 1] = new
+                    if colour == 1:
+                        RB[c, j] = left
             return carry
 
-        lax.fori_loop(0, 4, surround, 0)
-
-        for sweep in range(SWEEPS):
-            for colour in range(2):
-                last = sweep == SWEEPS - 1 and colour == 1
-
-                def update(big, carry, colour=colour, last=last):
-                    stores = []
-                    for small in range(GROUP):
-                        j = GROUP * big + small
-                        weights = [W[s, colour, j, k] for k in range(8)]
-                        for c in range(3):
-                            summed = total(s, colour, c, j, weights)
-                            new = summed * weights[7]
-                            left = summed - weights[6] * new if last else None
-                            stores.append((c, j, new, left))
-                    for c, j, new, left in stores:
-                        U[s, colour, c, j + 1] = new
-                        if last:
-                            RB[c, j] = left
-                    return carry
-
-                lax.fori_loop(0, EDGE // GROUP, update, 0)
-
-        taken = RIM[s, 48:56]
-
-        def finish(big, carry):
-            tiles = [[], [], [], [], [], []]
-            stores = []
-            for small in range(4):
-                j = 4 * big + small
-                weights = [W[s, 0, j, k] for k in range(7)]
-                for c in range(3):
-                    red, black = U[s, 0, c, j + 1], U[s, 1, c, j + 1]
-                    left = total(s, 0, c, j, weights) - weights[6] * red
-                    tiles[c].append(left + RB[c, j])
-                    tiles[3 + c].append(red + black)
-                    start = c * 1024 + 64 * j + s
-                    stores.append((start, jnp.where(even, red, black) * taken))
-                    stores.append((start + 32, jnp.where(even, black, red) * taken))
-            even_z = (third & 1) == 0
-            even_y = (quarter & 1) == 0
-            means = []
+        lax.fori_loop(0, SWEEPS, sweep, 0)
+
+
+        even_z = (third & 1) == 0
+        even_y = (quarter & 1) == 0
+        stores = []
+        for j in range(EDGE):
+            weights = [W[s, 0, j, k] for k in range(7)]
+            for c in range(3):
+                left = total(s, 0, c, j, weights) - weights[6] * U[s, 0, c, j + 1]
+                stores.append((c, j, left + RB[c, j]))
+        for c, j, left in stores:
+            RB[c, j] = left
+
+        stores = []
+        for big in range(4):
             for k in range(6):
+                tiles = []
+                for small in range(4):
+                    j = 4 * big + small
+                    if k < 3:
+                        tiles.append(RB[k, j])
+                    else:
+                        tiles.append(U[s, 0, k - 3, j + 1] + U[s, 1, k - 3, j + 1])
                 halves = []
                 for h in range(2):
-                    one, two = tiles[k][2 * h], tiles[k][2 * h + 1]
+                    one, two = tiles[2 * h], tiles[2 * h + 1]
                     halves.append(
                         jnp.where(
                             even_z, one + pltpu.roll(one, 127, 1), two + pltpu.roll(two, 1, 1)
                         )
                     )
-                means.append(
-                    0.125
-                    * jnp.where(
-                        even_y,
-                        halves[0] + pltpu.roll(halves[0], 96, 1),
-                        halves[1] + pltpu.roll(halves[1], 32, 1),
-                    )
+                mean = 0.125 * jnp.where(
+                    even_y,
+                    halves[0] + pltpu.roll(halves[0], 96, 1),
+                    halves[1] + pltpu.roll(halves[1], 32, 1),
                 )
-            for k in range(6):
-                MEAN[s, k, big] = means[k]
-            for start, tile in stores:
-                fo[pl.ds(start, 8, stride=SLOTS), :] = tile
-            return carry
-
-        lax.fori_loop(0, 4, finish, 0)
-
-        @pl.when(turn < peers)
-        def _():
-            push(
-                MEAN.at[s], RET.at[me], csend.at[turn - 1], crecv.at[turn - 1], {"gx": s}
-            ).start()
-
+                stores.append((6 * big + k, mean))
+        for number, mean in stores:
+            MEAN[s, number] = mean
+        for h in range(2):
+            index = (2 * h + ((lane & 3) >> 1)) * 32 + (lane & 1)
+            index = index + jnp.where(((lane >> 4) & 1) == 0, 30, 0)
+            end = jnp.zeros(TILE, jnp.float32)
+            for big in range(4):
+                for c in range(3):
+                    here = (quarter == c) & (((lane & 15) >> 2) == big)
+                    end = jnp.where(here, lane_take(MEAN[s, 6 * big + 3 + c], index), end)
+            ZM[s, pl.ds(h, 8, stride=2), :] = end
+
+        for way in range(6):
+            if way < 2 and turn == 1 + 2 * way:
+                RX[way, me] = MEAN[s, 21:24] if way == 0 else MEAN[s, 3:6]
+            else:
+                out_means.append(to_side(way, turn))
+                out_means[-1].start()
+        if turn > 0:
+            out_means.append(
+                push(
+                    MEAN.at[turn], RET.at[turn], csend.at[turn - 1], crecv.at[turn - 1],
+                    beside(0, -turn),
+                )
+            )
+            out_means[-1].start()
+
+    def to_side(way, turn):
+        sems = dsend.at[4 * way + turn], drecv.at[4 * way + turn]
+        step = 1 - 2 * (way & 1)
+        if way < 2:
+            tiles = MEAN.at[turn, 21:24] if way == 0 else MEAN.at[turn, 3:6]
+            return push(tiles, RX.at[way, me], *sems, beside(0, step - turn))
+        device = beside(way // 2, step) | beside(0, -turn)
+        if way < 4:
+            return push(MEAN.at[turn, :, 7 if way == 2 else 0], RY.at[way - 2, me], *sems, device)
+        return push(ZM.at[turn], RZ.at[way - 4, me], *sems, device)
+
+    out_means = []
+    for turn in (0, 2, 1, 3):
+        one_slot(turn)
+    RET[0] = MEAN[0]
+
+    def spell_out(j, carry):
+        for turn in range(SLOTS):
+            taken = RIM[turn, 48:56]
+            slot = lax.rem(me + (peers - turn), peers)
+            for c in range(3):
+                red, black = U[turn, 0, c, j + 1], U[turn, 1, c, j + 1]
+                start = c * 1024 + 64 * j + slot
+                rows = pl.ds(start, 8, stride=SLOTS)
+                fo[rows, :] = jnp.where(even, red, black) * taken
+                rows = pl.ds(start + 32, 8, stride=SLOTS)
+                fo[rows, :] = jnp.where(even, black, red) * taken
         return carry
 
-    lax.fori_loop(1, peers + 1, one_slot, 0)
-    RET[me] = MEAN[me]
-
+    lax.fori_loop(0, EDGE, spell_out, 0)
+    for facing in range(2):
+        for c in range(4):
+            C[c, facing * 17] = HX[facing, c]
+    loads[5].wait()
     for turn in range(1, peers):
-        owner_at = lax.rem(me + turn, peers)
         push(
-            MEAN.at[owner_at], RET.at[owner_at], csend.at[turn - 1], crecv.at[turn - 1], beside(0, 1)
+            MEAN.at[turn], RET.at[turn], csend.at[turn - 1], crecv.at[turn - 1], beside(0, -turn)
         ).wait_recv()
-
-    first_here = (lane >> 4) == positions[0]
-    second_here = (lane >> 4) == positions[1]
-
-    def spread(big, carry):
+    senders = [lax.rem(groups[i] + (peers - me), peers) for i in range(2)]
+    for i in range(2):
+        for number in range(24):
+            RS[i, number] = RET[senders[i], number]
+    for turn in range(peers):
+        for way in range(6):
+            if way < 2 and turn == 1 + 2 * way:
+                continue
+            step = 0 if way >= 2 else 2 * way - 1
+            owner_at = lax.rem(me + (turn + step + peers), peers)
+            sems = dsend.at[4 * way + turn], drecv.at[4 * way + turn]
+            if way < 2:
+                pair = MEAN.at[0, 0:3], RX.at[way, owner_at]
+            elif way < 4:
+                pair = MEAN.at[0, :, 0], RY.at[way - 2, owner_at]
+            else:
+                pair = ZM.at[0], RZ.at[way - 4, owner_at]
+            push(*pair, *sems, beside(1, 1)).wait_recv()
+
+    for copy in outward + out_rims + out_means:
+        copy.wait_send()
+
+
+def write_out(
+    fine, C, CR, HX, HY, HZ, RX, RY, RZ, RS, M, fo, so, ro, SP, RM, HYN, HZN, R, sem
+):
+    copies = [
+        pltpu.make_async_copy(SP.at[:, 1 : EDGE + 1], so, sem.at[0]),
+        pltpu.make_async_copy(fine, fo, sem.at[1]),
+        pltpu.make_async_copy(R, ro, sem.at[2]),
+    ]
+    copies[1].start()
+    lane = lax.broadcasted_iota(jnp.int32, TILE, 1)
+    refined = [M[i, 0:8] > 0.5 for i in range(2)]
+
+    def sources(small, h, lanes):
+        return (2 * h + (small >> 1)) * 32 + (small & 1) + 2 * (lanes & 15)
+
+    for big in range(4):
         stores = []
         for k in range(6):
-            first = RET[groups[0], k, big]
-            second = RET[groups[1], k, big]
+            first = RS[0, 6 * big + k]
+            second = RS[1, 6 * big + k]
             for small in range(4):
                 x = 4 * big + small
                 for h in range(2):
-                    index = (2 * h + (small >> 1)) * 32 + (small & 1) + 2 * (lane & 15)
+                    index = sources(small, h, lane)
                     rows = pl.ds(h, 8, stride=2)
-                    base = C[k - 3, x + 1, rows, :] if k >= 3 else jnp.zeros(TILE, jnp.float32)
-                    value = jnp.where(
-                        first_here,
-                        lane_take(first, index),
-                        jnp.where(second_here, lane_take(second, index), base),
-                    )
+                    value = jnp.where(refined[0], lane_take(first, index), lane_take(second, index))
+                    if k >= 3:
+                        base = C[k - 3, x + 1, rows, :]
+                        value = jnp.where(refined[0] | refined[1], value, base)
                     stores.append((k, x, rows, value))
         for k, x, rows, value in stores:
             if k >= 3:
                 SP[k - 3, x + 1, rows, :] = value
             else:
                 RM[k, x, rows, :] = value
-        return carry
-
-    lax.fori_loop(0, 4, spread, 0)
-
-    outward2 = faces(SP, pl.ds(1, EDGE), HX2, HY2, HZ2, ZF2, dsend, drecv)
-    for copy in outward2[:4]:
-        copy.start()
-    packed = jnp.zeros(SLAB, jnp.float32)
-    for c in range(3):
-        for x in range(EDGE):
-            plane = SP[c, x + 1]
-            low, high = 32 * c + x, 32 * c + 16 + x
-            packed = jnp.where(lane16 == low, pltpu.roll(plane, (low - 127) % 128, 1), packed)
-            packed = jnp.where(lane16 == high, pltpu.roll(plane, high, 1), packed)
-    ZF2[...] = packed
-    for copy in outward2[4:]:
-        copy.start()
-
+    copies[0].start()
+
+    def chosen(mark, base, values):
+        for number, value in enumerate(values):
+            base = jnp.where(mark == number + 1.0, value, base)
+        return base
+
+    stores = []
     for facing in range(2):
-        for c in range(4):
-            C[c, facing * 17] = HX[facing, c]
-    loads[5].wait()
-    for copy in outward2:
-        copy.wait_recv()
+        mark = HX[facing, 4, 0:8]
+        for h in range(2):
+            rows = pl.ds(h, 8, stride=2)
+            index = sources(3 - 3 * facing, h, lane)
+            for c in range(3):
+                values = [lane_take(RX[facing, number, c], index) for number in range(SLOTS)]
+                stores.append((facing, c, rows, chosen(mark, HX[facing, c, rows, :], values)))
+    for facing, c, rows, value in stores:
+        SP[c, facing * 17, rows, :] = value
+    tall = (24, 128)
     for facing in range(2):
-        outside = at[0] == (size[0] - 1 if facing else 0)
-        SP[:, facing * 17] = jnp.where(outside, 0.0, HX2[facing])
-        outside = at[1] == (size[1] - 1 if facing else 0)
-        HY2[facing] = jnp.where(outside, 0.0, HY2[facing])
-        outside = at[2] == (size[2] - 1 if facing else 0)
-        HZ2[facing] = jnp.where(outside, 0.0, HZ2[facing])
-
-    refined_here = (group16 == positions[0]) | (group16 == positions[1])
-    mask[...] = jnp.where(refined_here, 1.0, 0.0)
-    for copy in outward + out_rims + outward2:
-        copy.wait_send()
-    for turn in range(1, peers):
-        owner_at = lax.rem(me + turn, peers)
-        push(
-            MEAN.at[owner_at], RET.at[owner_at], csend.at[turn - 1], crecv.at[turn - 1], beside(0, 1)
-        ).wait_send()
-
-
-def write_out(
-    fine, C, CR, HY, HZ, SP, RM, HY2, HZ2, mask, fo, so, ro, R, sem
-):
-    copies = [
-        pltpu.make_async_copy(SP.at[:, 1 : EDGE + 1], so, sem.at[0]),
-        pltpu.make_async_copy(fine, fo, sem.at[1]),
-        pltpu.make_async_copy(R, ro, sem.at[2]),
-    ]
-    copies[0].start()
-    copies[1].start()
+        mark = jnp.broadcast_to(HY[facing, 4, 0:1], tall)
+        for small in range(4):
+            index = sources(small, 1 - facing, lax.broadcasted_iota(jnp.int32, tall, 1))
+            values = [lane_take(RY[facing, number], index) for number in range(SLOTS)]
+            HYN[facing, small] = chosen(mark, jnp.zeros(tall, jnp.float32), values)
+        HZN[facing] = chosen(
+            HZ[facing, 16:32], HZ[facing, 0:16], [RZ[facing, number] for number in range(SLOTS)]
+        )
+    near_refined = [HY[facing, 4] > 0.5 for facing in range(2)]
+
     lane16 = lax.broadcasted_iota(jnp.int32, SLAB, 1)
     row16 = lax.broadcasted_iota(jnp.int32, SLAB, 0)
-    refined_here = mask[...] > 0.5
-
-    def leftover(big, carry):
-        def neighbours(block, c, x, hy, hz):
+    refined_here = (M[0] + M[1]) > 0.5
+
+    def leftover(big):
+        def neighbours(block, c, x, hz):
             centre = block[c, x + 1]
             lanes = [
-                lane_take(hz[f], jnp.full(SLAB, 32 * c + 16 * f, jnp.int32) + x) for f in range(2)
+                lane_take(hz[f, 0:16], jnp.full(SLAB, 32 * c + 16 * f, jnp.int32) + x) for f in range(2)
             ]
-            rows = [jnp.broadcast_to(hy[f, c, pl.ds(x, 1), :], SLAB) for f in range(2)]
+            rows = [jnp.broadcast_to(HY[f, c, pl.ds(x, 1), :], SLAB) for f in range(2)]
+            if c < 3:
+                row = 6 * (x >> 2) + 3 + c
+                news = [HYN[f, x & 3, pl.ds(row, 1), :] for f in range(2)]
+                rows = [
+                    jnp.where(near_refined[f], jnp.broadcast_to(news[f], SLAB), rows[f])
+                    for f in range(2)
+                ]
             return centre, [
                 block[c, x],
                 block[c, x + 2],
@@ -518,12 +581,12 @@
             ]
 
         stores = []
-        for small in range(2):
-            x = 2 * big + small
-            centre, near = neighbours(C, 3, x, HY, HZ)
+        for small in range(8):
+            x = 8 * big + small
+            centre, near = neighbours(C, 3, x, HZ)
             face = [0.5 * (centre + value) for value in near]
             for c in range(3):
-                centre, near = neighbours(SP, c, x, HY2, HZ2)
+                centre, near = neighbours(SP, c, x, HZN)
                 applied = face[0] * (centre - near[0])
                 for k in range(1, 6):
                     applied = applied + face[k] * (centre - near[k])
@@ -531,9 +594,9 @@
                 stores.append((c, x, jnp.where(refined_here, RM[c, x], left)))
         for c, x, left in stores:
             R[c, x] = left
-        return carry
-
-    lax.fori_loop(0, EDGE // 2, leftover, 0)
+
+    for big in range(EDGE // 8):
+        leftover(big)
     copies[2].start()
     for copy in copies:
         copy.wait()
@@ -554,15 +617,16 @@
     here = lambda x: pltpu.with_memory_space_constraint(x, pltpu.HBM)
     kept = [
         (3072, 128),
-        (4, 18, 16, 128),
+        (5, 18, 16, 128),
         (3, 16, 16, 128),
+        (2, 5, 16, 128),
+        (2, 5, 16, 128),
+        (2, 32, 128),
+        (2, 4, 3, 8, 128),
+        (2, 4, 24, 128),
         (2, 4, 16, 128),
+        (2, 24, 8, 128),
         (2, 16, 128),
-        (3, 18, 16, 128),
-        (3, 16, 16, 128),
-        (2, 3, 16, 128),
-        (2, 16, 128),
-        (16, 128),
     ]
     held = pl.pallas_call(
         kernel,
@@ -575,8 +639,7 @@
             vmem(3072, 128),
             vmem(1024, 128),
             vmem(2, 4, 16, 128),
-            vmem(2, 4, 16, 128),
-            vmem(16, 128),
+            vmem(32, 128),
             vmem(4, 56, 128),
             vmem(4, 56, 128),
             vmem(4, 2, 18, 8, 128),
@@ -585,13 +648,12 @@
             vmem(4, 2, 16, 8, 8, 128),
             vmem(4, 16, 128),
             vmem(3, 16, 8, 128),
-            vmem(4, 6, 4, 8, 128),
-            vmem(4, 6, 4, 8, 128),
-            vmem(2, 3, 16, 128),
-            vmem(16, 128),
+            vmem(4, 24, 8, 128),
+            vmem(4, 24, 8, 128),
+            vmem(4, 16, 128),
             pltpu.SMEM((1, 2), jnp.int32),
             pltpu.SMEM((1, 2), jnp.int32),
-            dma(8), dma(6), dma(6), dma(3), dma(3), dma(3), dma(3), dma(6), dma(6),
+            dma(8), dma(6), dma(6), dma(3), dma(3), dma(3), dma(3), dma(24), dma(24),
         ],
         compiler_params=pltpu.CompilerParams(
             collective_id=0, has_side_effects=True, vmem_limit_bytes=48 * 2**20
@@ -611,7 +673,14 @@
         ],
         in_specs=[in_vmem] * len(kept),
         out_specs=[any_space] * 3,
-        scratch_shapes=[vmem(3, 16, 16, 128), dma(3)],
+        scratch_shapes=[
+            vmem(3, 18, 16, 128),
+            vmem(3, 16, 16, 128),
+            vmem(2, 4, 24, 128),
+            vmem(2, 16, 128),
+            vmem(3, 16, 16, 128),
+            dma(3),
+        ],
     )(*(pltpu.with_memory_space_constraint(x, pltpu.VMEM) for x in held))
     fine = fine.reshape(3, 256, SLOTS, 128).transpose(0, 2, 1, 3).reshape(3, SLOTS, 32768)
     return fine.transpose(1, 0, 2)[None], synced, residual

time: 32.7 us -> 29.9 us (0.914)
  Pallas kernels: 31.9 us -> 29 us
    pallas_call x1, Pallas kernels: 29.6 us -> 26.1 us  [shards(): pl.pallas_call(kernel, name='smooth', out_shape=[vmem(*dims) for dims in...]
    pallas_call x1, Pallas kernels: 2.33 us -> 2.88 us  [shards(): pl.pallas_call(write_out, name='write_out', out_shape=[shape((3072, 128),...]
where the time goes in v3:
time: 29.9 us; the launch traced here: 29.6 us
  Pallas kernels  29 us (97%)
  between operations  0.64 us (2%)
    pallas_call x1, Pallas kernels, shards(): pl.pallas_call(kernel, name='smooth', out_shape=[vmem(*dims) for dims in...  26.1 us
    pallas_call x1, Pallas kernels, shards(): pl.pallas_call(write_out, name='write_out', out_shape=[shape((3072, 128),...  2.88 us

profile of v3, /device:TPU:1, one launch (start us, length us, event | category | flops | bytes accessed | tf_op | source)
XLA Modules:
  0.0 29.6 jit_solution(4964349909299389044)
XLA Ops:
  0.6 26.1 %smooth.1 = (f32[3072,128]{1,0:T(8,128)S(1)}, f32[5,18,16,128]{3,2,1,0:T(8,128)S(1)}, f32[3,16,16,128]{3,2,1,0:T(8,128)S(1)}, f32[2,5,16,128]{3,2,1,0:T(8,128)S(...) custom-call(f32[3,16,16,128]{3,2,1,0:T(8,128)} %cv.1, ...), custom_call_target="tpu_custom_call" | custom-call | tf_op jit(solution)/shard_map/smooth/pallas_call | solution.py:631
  26.7 2.9 %write_out.1 = (f32[3072,128]{1,0:T(8,128)}, f32[3,16,16,128]{3,2,1,0:T(8,128)}, f32[3,16,16,128]{3,2,1,0:T(8,128)}) custom-call(f32[3072,128]{1,0:T(8,128)S(1)} %get-tuple-element.17.fine, f32[5,18,16,128]{3,2,1,0:T(8,128)S(1)} %get-tuple-element.18.C, f32[3,16,16,128]{3,2,1,0:T(8,128)S(1)} %get-tuple-element.19.CR, ...), custom_call_target="tpu_custom_call" | custom-call | tf_op jit(solution)/shard_map/write_out/pallas_call | solution.py:666

commit v4 on v3

--- a/solution.py
+++ b/solution.py
@@ -47,9 +47,9 @@
 
 def kernel(
     cv, cm, cr, fv, fr, fm, place_in, own_in,
-    fo, C, CR, HX, HY, HZ, RX, RY, RZ, RS, M,
+    fo, C, CR, HX, HY, HZ, RX, RY, RZ, RSV, RSR, M,
     FV, FR, FM, EF, ZF, MSG, RIM, PV, U, LD, W, GY, RB,
-    MEAN, RET, ZM, place, own,
+    MV, MR, RETV, RETR, ZM, place, own,
     lsem, asend, arecv, bsend, brecv, csend, crecv, dsend, drecv,
 ):
     at = [lax.axis_index(axis) for axis in AXES]
@@ -73,9 +73,7 @@
         loads[number].start()
 
     barrier = pltpu.get_barrier_semaphore()
-    for step in range(1, peers):
-        pl.semaphore_signal(barrier, inc=1, device_id=beside(0, step), device_id_type=MESH)
-    for number in (1, 2):
+    for number in range(3):
         for step in (1, -1):
             pl.semaphore_signal(
                 barrier, inc=1, device_id=beside(number, step), device_id_type=MESH
@@ -129,7 +127,7 @@
         packed = jnp.where(group16 == 2 * c, pltpu.roll(upper, turn, 1), packed)
         packed = jnp.where(group16 == 2 * c + 1, pltpu.roll(lower, turn, 1), packed)
     ZF[0:16] = packed
-    pl.semaphore_wait(barrier, peers + 3)
+    pl.semaphore_wait(barrier, 6)
     inner = pl.ds(1, EDGE)
     outward = [
         push(C.at[:, EDGE], HX.at[0], asend.at[0], arecv.at[0], beside(0, 1)),
@@ -157,7 +155,8 @@
             PV[s, 0, j + 1], PV[s, 1, j + 1] = pair(FM, slot)
             for c in range(3):
                 LD[s, 0, c, j], LD[s, 1, c, j] = pair(FR, c * 1024 + slot)
-                U[s, 0, c, j + 1], U[s, 1, c, j + 1] = pair(FV, c * 1024 + slot)
+                rows = pl.ds(pl.multiple_of(8 * j + 8, 8), 8)
+                U[s, 0, c, rows], U[s, 1, c, rows] = pair(FV, c * 1024 + slot)
         return carry
 
     def y_up(tile):
@@ -262,13 +261,15 @@
 
     def total(s, colour, c, j, weights):
         other = U.at[s, 1 - colour, c]
-        tile = other[j + 1]
+        at_row = 8 * j + 8
+        tile = other[at_row : at_row + 8]
+        behind, ahead = other[at_row - 1 : at_row + 7], other[at_row + 1 : at_row + 9]
         return (
             LD[s, colour, c, j]
             + weights[0] * tile
-            + weights[1] * far(colour, other[j], other[j + 2])
-            + weights[2] * y_down(tile)
-            + weights[3] * y_up(tile)
+            + weights[1] * far(colour, other[at_row - 8 : at_row], other[at_row + 8 : at_row + 16])
+            + weights[2] * pltpu.roll(jnp.where(quarter == 3, behind, tile), 32, 1)
+            + weights[3] * pltpu.roll(jnp.where(quarter == 0, ahead, tile), 96, 1)
             + weights[4] * pltpu.roll(tile, 1, 1)
             + weights[5] * pltpu.roll(tile, 127, 1)
         )
@@ -295,7 +296,7 @@
                     rim_x.append(ghost)
                 else:
                     for colour in range(2):
-                        U[s, colour, c, facing * 17] = ghost
+                        U[s, colour, c, facing * 136 : facing * 136 + 8] = ghost
             index = 32 * c + jnp.where((lane16 >> 5) == 3, 16, 0) + ((lane16 & 31) >> 1)
             GY[c] = lane_take(y_slab, index)
         for colour in range(2):
@@ -357,7 +358,7 @@
                         left = summed - weights[6] * new if colour == 1 else None
                         stores.append((c, j, new, left))
                 for c, j, new, left in stores:
-                    U[s, colour, c, j + 1] = new
+                    U[s, colour, c, 8 * j + 8 : 8 * j + 16] = new
                     if colour == 1:
                         RB[c, j] = left
             return carry
@@ -367,41 +368,34 @@
 
         even_z = (third & 1) == 0
         even_y = (quarter & 1) == 0
-        stores = []
-        for j in range(EDGE):
-            weights = [W[s, 0, j, k] for k in range(7)]
+        def mean_of(tiles):
+            halves = []
+            for h in range(2):
+                one, two = tiles[2 * h], tiles[2 * h + 1]
+                halves.append(
+                    jnp.where(even_z, one + pltpu.roll(one, 127, 1), two + pltpu.roll(two, 1, 1))
+                )
+            return 0.125 * jnp.where(
+                even_y,
+                halves[0] + pltpu.roll(halves[0], 96, 1),
+                halves[1] + pltpu.roll(halves[1], 32, 1),
+            )
+
+        def to_home(tiles, back, number):
+            sems = csend.at[number], crecv.at[number]
+            out_means.append(push(tiles.at[turn], back.at[turn], *sems, beside(0, -turn)))
+            out_means[-1].start()
+
+        means = []
+        for big in range(4):
             for c in range(3):
-                left = total(s, 0, c, j, weights) - weights[6] * U[s, 0, c, j + 1]
-                stores.append((c, j, left + RB[c, j]))
-        for c, j, left in stores:
-            RB[c, j] = left
-
-        stores = []
-        for big in range(4):
-            for k in range(6):
                 tiles = []
-                for small in range(4):
-                    j = 4 * big + small
-                    if k < 3:
-                        tiles.append(RB[k, j])
-                    else:
-                        tiles.append(U[s, 0, k - 3, j + 1] + U[s, 1, k - 3, j + 1])
-                halves = []
-                for h in range(2):
-                    one, two = tiles[2 * h], tiles[2 * h + 1]
-                    halves.append(
-                        jnp.where(
-                            even_z, one + pltpu.roll(one, 127, 1), two + pltpu.roll(two, 1, 1)
-                        )
-                    )
-                mean = 0.125 * jnp.where(
-                    even_y,
-                    halves[0] + pltpu.roll(halves[0], 96, 1),
-                    halves[1] + pltpu.roll(halves[1], 32, 1),
-                )
-                stores.append((6 * big + k, mean))
-        for number, mean in stores:
-            MEAN[s, number] = mean
+                for j in range(4 * big, 4 * big + 4):
+                    rows = slice(8 * j + 8, 8 * j + 16)
+                    tiles.append(U[s, 0, c, rows] + U[s, 1, c, rows])
+                means.append(mean_of(tiles))
+        for number, mean in enumerate(means):
+            MV[s, number] = mean
         for h in range(2):
             index = (2 * h + ((lane & 3) >> 1)) * 32 + (lane & 1)
             index = index + jnp.where(((lane >> 4) & 1) == 0, 30, 0)
@@ -409,46 +403,60 @@
             for big in range(4):
                 for c in range(3):
                     here = (quarter == c) & (((lane & 15) >> 2) == big)
-                    end = jnp.where(here, lane_take(MEAN[s, 6 * big + 3 + c], index), end)
+                    end = jnp.where(here, lane_take(means[3 * big + c], index), end)
             ZM[s, pl.ds(h, 8, stride=2), :] = end
 
         for way in range(6):
             if way < 2 and turn == 1 + 2 * way:
-                RX[way, me] = MEAN[s, 21:24] if way == 0 else MEAN[s, 3:6]
+                RX[way, me] = MV[s, 9:12] if way == 0 else MV[s, 0:3]
             else:
                 out_means.append(to_side(way, turn))
                 out_means[-1].start()
         if turn > 0:
-            out_means.append(
-                push(
-                    MEAN.at[turn], RET.at[turn], csend.at[turn - 1], crecv.at[turn - 1],
-                    beside(0, -turn),
-                )
-            )
-            out_means[-1].start()
+            to_home(MV, RETV, turn - 1)
+
+        stores = []
+        for j in range(EDGE):
+            weights = [W[s, 0, j, k] for k in range(7)]
+            for c in range(3):
+                red = U[s, 0, c, 8 * j + 8 : 8 * j + 16]
+                left = total(s, 0, c, j, weights) - weights[6] * red
+                stores.append((c, j, left + RB[c, j]))
+        for c, j, left in stores:
+            RB[c, j] = left
+        means = []
+        for big in range(4):
+            for c in range(3):
+                means.append(mean_of([RB[c, 4 * big + i] for i in range(4)]))
+        for number, mean in enumerate(means):
+            MR[s, number] = mean
+        if turn > 0:
+            to_home(MR, RETR, turn + 2)
 
     def to_side(way, turn):
         sems = dsend.at[4 * way + turn], drecv.at[4 * way + turn]
         step = 1 - 2 * (way & 1)
         if way < 2:
-            tiles = MEAN.at[turn, 21:24] if way == 0 else MEAN.at[turn, 3:6]
+            tiles = MV.at[turn, 9:12] if way == 0 else MV.at[turn, 0:3]
             return push(tiles, RX.at[way, me], *sems, beside(0, step - turn))
         device = beside(way // 2, step) | beside(0, -turn)
         if way < 4:
-            return push(MEAN.at[turn, :, 7 if way == 2 else 0], RY.at[way - 2, me], *sems, device)
+            return push(MV.at[turn, :, 7 if way == 2 else 0], RY.at[way - 2, me], *sems, device)
         return push(ZM.at[turn], RZ.at[way - 4, me], *sems, device)
 
     out_means = []
-    for turn in (0, 2, 1, 3):
+    for turn in (0, 3, 2, 1):
         one_slot(turn)
-    RET[0] = MEAN[0]
+    RETV[0] = MV[0]
+    RETR[0] = MR[0]
 
     def spell_out(j, carry):
         for turn in range(SLOTS):
             taken = RIM[turn, 48:56]
             slot = lax.rem(me + (peers - turn), peers)
             for c in range(3):
-                red, black = U[turn, 0, c, j + 1], U[turn, 1, c, j + 1]
+                rows = pl.ds(pl.multiple_of(8 * j + 8, 8), 8)
+                red, black = U[turn, 0, c, rows], U[turn, 1, c, rows]
                 start = c * 1024 + 64 * j + slot
                 rows = pl.ds(start, 8, stride=SLOTS)
                 fo[rows, :] = jnp.where(even, red, black) * taken
@@ -462,13 +470,14 @@
             C[c, facing * 17] = HX[facing, c]
     loads[5].wait()
     for turn in range(1, peers):
-        push(
-            MEAN.at[turn], RET.at[turn], csend.at[turn - 1], crecv.at[turn - 1], beside(0, -turn)
-        ).wait_recv()
+        for tiles, back, number in ((MV, RETV, turn - 1), (MR, RETR, turn + 2)):
+            sems = csend.at[number], crecv.at[number]
+            push(tiles.at[turn], back.at[turn], *sems, beside(0, -turn)).wait_recv()
     senders = [lax.rem(groups[i] + (peers - me), peers) for i in range(2)]
     for i in range(2):
-        for number in range(24):
-            RS[i, number] = RET[senders[i], number]
+        for number in range(12):
+            RSV[i, number] = RETV[senders[i], number]
+            RSR[i, number] = RETR[senders[i], number]
     for turn in range(peers):
         for way in range(6):
             if way < 2 and turn == 1 + 2 * way:
@@ -477,9 +486,9 @@
             owner_at = lax.rem(me + (turn + step + peers), peers)
             sems = dsend.at[4 * way + turn], drecv.at[4 * way + turn]
             if way < 2:
-                pair = MEAN.at[0, 0:3], RX.at[way, owner_at]
+                pair = MV.at[0, 0:3], RX.at[way, owner_at]
             elif way < 4:
-                pair = MEAN.at[0, :, 0], RY.at[way - 2, owner_at]
+                pair = MV.at[0, :, 0], RY.at[way - 2, owner_at]
             else:
                 pair = ZM.at[0], RZ.at[way - 4, owner_at]
             push(*pair, *sems, beside(1, 1)).wait_recv()
@@ -489,7 +498,7 @@
 
 
 def write_out(
-    fine, C, CR, HX, HY, HZ, RX, RY, RZ, RS, M, fo, so, ro, SP, RM, HYN, HZN, R, sem
+    fine, C, CR, HX, HY, HZ, RX, RY, RZ, RSV, RSR, M, fo, so, ro, SP, RM, HYN, HZN, R, sem
 ):
     copies = [
         pltpu.make_async_copy(SP.at[:, 1 : EDGE + 1], so, sem.at[0]),
@@ -506,8 +515,8 @@
     for big in range(4):
         stores = []
         for k in range(6):
-            first = RS[0, 6 * big + k]
-            second = RS[1, 6 * big + k]
+            held, number = (RSV, 3 * big + k - 3) if k >= 3 else (RSR, 3 * big + k)
+            first, second = held[0, number], held[1, number]
             for small in range(4):
                 x = 4 * big + small
                 for h in range(2):
@@ -541,13 +550,13 @@
                 stores.append((facing, c, rows, chosen(mark, HX[facing, c, rows, :], values)))
     for facing, c, rows, value in stores:
         SP[c, facing * 17, rows, :] = value
-    tall = (24, 128)
     for facing in range(2):
-        mark = jnp.broadcast_to(HY[facing, 4, 0:1], tall)
+        mark = HY[facing, 4, 0:8]
         for small in range(4):
-            index = sources(small, 1 - facing, lax.broadcasted_iota(jnp.int32, tall, 1))
-            values = [lane_take(RY[facing, number], index) for number in range(SLOTS)]
-            HYN[facing, small] = chosen(mark, jnp.zeros(tall, jnp.float32), values)
+            index = sources(small, 1 - facing, lane)
+            for part in (slice(0, 8), slice(4, 12)):
+                values = [lane_take(RY[facing, number, part], index) for number in range(SLOTS)]
+                HYN[facing, small, part] = chosen(mark, jnp.zeros(TILE, jnp.float32), values)
         HZN[facing] = chosen(
             HZ[facing, 16:32], HZ[facing, 0:16], [RZ[facing, number] for number in range(SLOTS)]
         )
@@ -565,8 +574,8 @@
             ]
             rows = [jnp.broadcast_to(HY[f, c, pl.ds(x, 1), :], SLAB) for f in range(2)]
             if c < 3:
-                row = 6 * (x >> 2) + 3 + c
-                news = [HYN[f, x & 3, pl.ds(row, 1), :] for f in range(2)]
+                row = 3 * (x >> 2) + c
+                news = [HYN[f, x & 3, row : row + 1, :] for f in range(2)]
                 rows = [
                     jnp.where(near_refined[f], jnp.broadcast_to(news[f], SLAB), rows[f])
                     for f in range(2)
@@ -623,9 +632,10 @@
         (2, 5, 16, 128),
         (2, 32, 128),
         (2, 4, 3, 8, 128),
-        (2, 4, 24, 128),
+        (2, 4, 12, 128),
         (2, 4, 16, 128),
-        (2, 24, 8, 128),
+        (2, 12, 8, 128),
+        (2, 12, 8, 128),
         (2, 16, 128),
     ]
     held = pl.pallas_call(
@@ -643,17 +653,19 @@
             vmem(4, 56, 128),
             vmem(4, 56, 128),
             vmem(4, 2, 18, 8, 128),
-            vmem(4, 2, 3, 18, 8, 128),
+            vmem(4, 2, 3, 144, 128),
             vmem(4, 2, 3, 16, 8, 128),
             vmem(4, 2, 16, 8, 8, 128),
             vmem(4, 16, 128),
             vmem(3, 16, 8, 128),
-            vmem(4, 24, 8, 128),
-            vmem(4, 24, 8, 128),
+            vmem(4, 12, 8, 128),
+            vmem(4, 12, 8, 128),
+            vmem(4, 12, 8, 128),
+            vmem(4, 12, 8, 128),
             vmem(4, 16, 128),
             pltpu.SMEM((1, 2), jnp.int32),
             pltpu.SMEM((1, 2), jnp.int32),
-            dma(8), dma(6), dma(6), dma(3), dma(3), dma(3), dma(3), dma(24), dma(24),
+            dma(8), dma(6), dma(6), dma(3), dma(3), dma(6), dma(6), dma(24), dma(24),
         ],
         compiler_params=pltpu.CompilerParams(
             collective_id=0, has_side_effects=True, vmem_limit_bytes=48 * 2**20
@@ -676,7 +688,7 @@
         scratch_shapes=[
             vmem(3, 18, 16, 128),
             vmem(3, 16, 16, 128),
-            vmem(2, 4, 24, 128),
+            vmem(2, 4, 16, 128),
             vmem(2, 16, 128),
             vmem(3, 16, 16, 128),
             dma(3),

time: 29.9 us -> 28 us (0.936)
  Pallas kernels: 29 us -> 27.2 us
    pallas_call x1, Pallas kernels: 26.1 us -> 24.4 us  [shards(): pl.pallas_call(kernel, name='smooth', out_shape=[vmem(*dims) for dims in...]
where the time goes in v4:
time: 28 us; the launch traced here: 27.9 us
  Pallas kernels  27.2 us (97%)
  between operations  0.64 us (2%)
    pallas_call x1, Pallas kernels, shards(): pl.pallas_call(kernel, name='smooth', out_shape=[vmem(*dims) for dims in...  24.4 us
    pallas_call x1, Pallas kernels, shards(): pl.pallas_call(write_out, name='write_out', out_shape=[shape((3072, 128),...  2.85 us

profile of v4, /device:TPU:1, one launch (start us, length us, event | category | flops | bytes accessed | tf_op | source)
XLA Modules:
  0.0 27.9 jit_solution(8375683395757138982)
XLA Ops:
  0.6 24.4 %smooth.1 = (f32[3072,128]{1,0:T(8,128)S(1)}, f32[5,18,16,128]{3,2,1,0:T(8,128)S(1)}, f32[3,16,16,128]{3,2,1,0:T(8,128)S(1)}, f32[2,5,16,128]{3,2,1,0:T(8,128)S(...) custom-call(f32[3,16,16,128]{3,2,1,0:T(8,128)} %cv.1, ...), custom_call_target="tpu_custom_call" | custom-call | tf_op jit(solution)/shard_map/smooth/pallas_call | solution.py:641
  25.0 2.9 %write_out.1 = (f32[3072,128]{1,0:T(8,128)}, f32[3,16,16,128]{3,2,1,0:T(8,128)}, f32[3,16,16,128]{3,2,1,0:T(8,128)}) custom-call(f32[3072,128]{1,0:T(8,128)S(1)} %get-tuple-element.18.fine, f32[5,18,16,128]{3,2,1,0:T(8,128)S(1)} %get-tuple-element.19.C, f32[3,16,16,128]{3,2,1,0:T(8,128)S(1)} %get-tuple-element.20.CR, ...), custom_call_target="tpu_custom_call" | custom-call | tf_op jit(solution)/shard_map/write_out/pallas_call | solution.py:678
